TPU v7x, 256 devices: a whole 4x4x8 slice. The times are simulated.
256 devices in a mesh: cube: 64 (over y, z_lo, x, core), panel: 4 (over z_hi).
Axes of the slice: x: 4, y: 4, z: 8 (z_hi: 4, z_lo: 2; z = z_hi * 2 + z_lo), core: 2. Of those that a mesh axis runs over, the one named last changes fastest.
Arguments:
- leaf_updates: float32 [32768, 4096], P(('cube', 'panel')), as said below
- extend_maps: int32 [14, 4096], replicated, may hold values from 0 to 4607, as said below
- front_diagonal: float32 [7, 4608], replicated, may hold values from 0.5 to 2
- pivot_order: int32 [512], replicated, may hold values from 0 to 511, each once
- coupling_rows: bfloat16 [65536, 4608], P(('cube', 'panel')), may hold values from -0.1796875 to 0.1796875
- coupling_owner: int32 [65536, 1], P(('cube', 'panel')), may hold values from 0 to 255; in each aligned block of 256 rows (0 to 255, 256 to 511, ...) at most 2 rows name the same one
- coupling_slot: int32 [65536], P(('cube', 'panel')), may hold values from 0 to 15
Outputs:
- root_factor: bfloat16 [4096, 512], P(('cube', 'panel'))
- root_update: float32 [4096, 4096], P(('cube', 'panel'))
Inputs may be any that keep to these rules, and one draw needn't show every extreme that they name: leaf_updates: each of the 8 blocks of 4096 rows is symmetric positive definite. `extend_maps`: each row names distinct indices. For a child h of its parent (h = row parity) at merge level j, with g = 8 * 2 ** j, r = 4096 // (2 * g * 4) and k = 512 // (2 * g * 4): its indices fall in aligned blocks of 2 * r, block number s * 4 + p; the first r of a block name front indices of parent block (h * g + s) * 4 + p, the other r those of parent block ((1 - h) * g + s) * 4 + p, where parent block u holds pivots u * k to u * k + k - 1 and indices 512 + u * r to 512 + u * r + r - 1. `coupling_owner`: within the rows of one device, no owner is named by more than 2 rows.
All inputs are finite; a program needn't handle non-finite values.
Results may differ from a plain program's by a relative error of at most 0.0065.
Values may be sent and summed in bfloat16 or wider, within the bound.
A program may use at most 128 MiB of HBM per device.

v0:
```python
import jax
import jax.numpy as jnp
from jax import lax
from jax.sharding import PartitionSpec as P

CAP = 2


def from_partner(shard, axis, stride):
    return lax.ppermute(shard, axis, [(i, i ^ 1 << stride) for i in range(lax.axis_size(axis))])


def route_rows(coupling_rows, coupling_owner, coupling_slot, cubes, panels, root_rows):
    owners = coupling_owner[:, 0]
    owner_count = cubes * panels
    owner_hits = (owners[:, None] == jnp.arange(owner_count, dtype=jnp.int32)[None, :]).astype(
        jnp.int32
    )
    earlier = jnp.sum((jnp.cumsum(owner_hits, axis=0) - owner_hits) * owner_hits, axis=1)
    target = owners * CAP + earlier
    row_width = coupling_rows.shape[1]
    outgoing = jnp.zeros((owner_count * CAP, row_width), jnp.bfloat16).at[target].set(coupling_rows)
    slot_marks = (coupling_slot[:, None] == jnp.arange(root_rows, dtype=jnp.int32)[None, :]).astype(
        jnp.bfloat16
    )
    labels = jnp.zeros((owner_count * CAP, root_rows), jnp.bfloat16).at[target].set(slot_marks)
    outgoing = outgoing.reshape(cubes, panels, CAP, row_width)
    labels = labels.reshape(cubes, panels, CAP, root_rows)
    got_rows, got_labels = (
        lax.all_to_all(
            lax.all_to_all(outgoing, "cube", split_axis=0, concat_axis=0, tiled=True),
            "panel",
            split_axis=1,
            concat_axis=1,
            tiled=True,
        ),
        lax.all_to_all(
            lax.all_to_all(labels, "cube", split_axis=0, concat_axis=0, tiled=True),
            "panel",
            split_axis=1,
            concat_axis=1,
            tiled=True,
        ),
    )
    return jnp.einsum("abcr,abcf->rf", got_labels, got_rows, preferred_element_type=jnp.float32)


def place_rows(
    child_rows, child_map, block_start, parent_block, piv_rows, upd_rows, pivots, order_full
):
    targets = lax.dynamic_slice_in_dim(child_map, block_start, upd_rows)
    slots = jnp.where(
        targets < pivots,
        targets - parent_block * piv_rows,
        piv_rows + targets - pivots - parent_block * upd_rows,
    )
    source = (
        jnp.full((piv_rows + upd_rows,), -1, jnp.int32)
        .at[slots]
        .set(jnp.arange(upd_rows, dtype=jnp.int32))
    )
    columns = (
        jnp.full((order_full,), -1, jnp.int32)
        .at[child_map]
        .set(jnp.arange(child_map.shape[0], dtype=jnp.int32))
    )
    picked = jnp.take(child_rows, jnp.maximum(source, 0), axis=0)
    picked = jnp.take(picked, jnp.maximum(columns, 0), axis=1)
    present = (source >= 0)[:, None] & (columns >= 0)[None, :]
    return jnp.where(present, picked, 0.0)


def pair_join(mine, partner, cube_at, bit_step):
    upper_half = cube_at // 2**bit_step % 2
    return jnp.where(
        upper_half == 0, jnp.concatenate([mine, partner], 0), jnp.concatenate([partner, mine], 0)
    )


def body(
    leaf_updates,
    extend_maps,
    front_diagonal,
    pivot_order,
    coupling_rows,
    coupling_owner,
    coupling_slot,
):
    cubes = lax.axis_size("cube")
    panels = lax.axis_size("panel")
    cube_bits = cubes.bit_length() - 1
    cube_at = lax.axis_index("cube")
    panel_at = lax.axis_index("panel")
    row_width = leaf_updates.shape[1]
    pivots = pivot_order.shape[0]
    order_full = front_diagonal.shape[1]
    assembly = route_rows(
        coupling_rows, coupling_owner, coupling_slot, cubes, panels, row_width // (cubes * panels)
    )
    columns_all = jnp.arange(order_full, dtype=jnp.int32)
    children = leaf_updates
    map_base = 0
    diag_base = 0
    factor = None
    for merge_level in range(3):
        level_bit = cube_bits - 3 + merge_level
        group_size = 2 ** (level_bit + 1)
        half_group = group_size // 2
        position = cube_at % group_size
        front_at = cube_at // group_size
        child_side = position // half_group
        lower_pos = position % half_group
        upd_rows = row_width // (group_size * panels)
        piv_rows = pivots // (group_size * panels)
        child_block = lower_pos * panels + panel_at
        parent_block = position * panels + panel_at
        incoming = from_partner(children[upd_rows:], "cube", level_bit)
        own_map = jnp.take(extend_maps, map_base + 2 * front_at + child_side, axis=0)
        other_map = jnp.take(extend_maps, map_base + 2 * front_at + 1 - child_side, axis=0)
        block_start = child_block * 2 * upd_rows
        front_rows = place_rows(
            children[:upd_rows],
            own_map,
            block_start,
            parent_block,
            piv_rows,
            upd_rows,
            pivots,
            order_full,
        )
        front_rows = front_rows + place_rows(
            incoming,
            other_map,
            block_start + upd_rows,
            parent_block,
            piv_rows,
            upd_rows,
            pivots,
            order_full,
        )
        slot_ids = jnp.arange(piv_rows + upd_rows, dtype=jnp.int32)
        global_rows = jnp.where(
            slot_ids < piv_rows,
            parent_block * piv_rows + slot_ids,
            pivots + parent_block * upd_rows + slot_ids - piv_rows,
        )
        diag_row = jnp.take(front_diagonal, diag_base + front_at, axis=0)
        front_rows = front_rows + jnp.where(
            columns_all[None, :] == global_rows[:, None],
            jnp.take(diag_row, global_rows)[:, None],
            0.0,
        )
        pivot_rows = front_rows[:piv_rows, :pivots]
        update_rows = front_rows[piv_rows:]
        if merge_level == 2:
            update_rows = update_rows + assembly
        pivot_block = lax.all_gather(pivot_rows, "panel", axis=0, tiled=True)
        for bit_step in range(level_bit + 1):
            partner = from_partner(pivot_block, "cube", bit_step)
            pivot_block = pair_join(pivot_block, partner, cube_at, bit_step)
        coupled = update_rows[:, :pivots]
        if merge_level == 2:
            pivot_block = jnp.take(jnp.take(pivot_block, pivot_order, axis=0), pivot_order, axis=1)
            coupled = jnp.take(coupled, pivot_order, axis=1)
        chol_lower = jnp.linalg.cholesky(pivot_block)
        factor = lax.linalg.triangular_solve(
            chol_lower, coupled, left_side=False, lower=True, transpose_a=True
        ).astype(jnp.bfloat16)
        contract = (((1,), (1,)), ((), ()))
        collected = lax.all_gather(factor, "panel", axis=0, tiled=True)
        for bit_step in range(level_bit + 1):
            partner = from_partner(collected, "cube", bit_step)
            collected = pair_join(collected, partner, cube_at, bit_step)
        product = lax.dot_general(factor, collected, contract, preferred_element_type=jnp.float32)
        children = update_rows[:, pivots:] - product
        map_base += 8 // 2**merge_level
        diag_base += 4 // 2**merge_level
    return (factor, children)


def solution(mesh):
    return jax.shard_map(
        body,
        mesh=mesh,
        in_specs=(
            P(("cube", "panel"), None),
            P(),
            P(),
            P(),
            P(("cube", "panel"), None),
            P(("cube", "panel"), None),
            P(("cube", "panel")),
        ),
        out_specs=(P(("cube", "panel"), None), P(("cube", "panel"), None)),
        check_vma=False,
    )
```

profile of v0, /device:TPU:1, one launch (start us, length us, event | category | flops | bytes accessed | tf_op | source)
XLA Modules:
  0.0 1199.4 jit_solution(4935917101445240276)
XLA Ops:
  8.1 15.5 %scatter_custom_fusion.5 = s32[4608]{0:T(1024)S(1)} fusion(s32[4096]{0:T(1024)S(1)} %compare_select_fusion.3, s32[4096]{0:T(1024)S(1)} %iota.179, s32[]{:T(128)} %constant.591.clone.1), kind=kCustom, calls=%fused_computation.332 | custom fusion | bytes 18436 | tf_op jit(solution)/shard_map/scatter | solution.py:65
  40.6 15.5 %scatter_custom_fusion.7 = s32[4608]{0:T(1024)S(1)} fusion(s32[4096]{0:T(1024)S(1)} %compare_select_fusion.2, s32[4096]{0:T(1024)S(1)} %iota.181, s32[]{:T(128)} %constant.591.clone.1), kind=kCustom, calls=%fused_computation.330 | custom fusion | bytes 18436 | tf_op jit(solution)/shard_map/scatter | solution.py:65
  80.0 13.8 %all_gather.18 = f32[32,512]{1,0:T(8,128)S(1)} all-gather(f32[8,512]{1,0:T(8,128)S(1)} %slice.288), channel_id=1, replica_groups=mesh['cube'=64,'panel'=4] {'panel'}, dimensions={0}, use_global_device_ids=true | all-gather | bytes 81920 | tf_op jit(solution)/shard_map/all_gather | solution.py:157
  128.3 11.7 cholesky.374
  152.5 11.7 cholesky.393
  177.2 11.7 cholesky.414
  200.8 11.7 cholesky.431
  225.0 39.3 %custom-call.29 = f32[4,128,128]{1,2,0:T(8,128)S(1)} custom-call(f32[4,128,128]{2,1,0:T(8,128)S(1)} %get-tuple-element.34), custom_call_target="InvertDiagBlocksLowerTriangular" | custom-call | tf_op jit(solution)/shard_map/triangular_solve | solution.py:166
  269.1 12.4 %all_gather.19 = bf16[256,512]{1,0:T(8,128)(2,1)S(1)} all-gather(bf16[64,512]{1,0:T(8,128)(2,1)S(1)} %pad_maximum_fusion), channel_id=1, replica_groups=mesh['cube'=64,'panel'=4] {'panel'}, dimensions={0}, use_global_device_ids=true | all-gather | bytes 327680 | tf_op jit(solution)/shard_map/all_gather | solution.py:170
  289.7 11.9 collective-permute-done.6
  305.7 15.5 %scatter_custom_fusion.3 = s32[4608]{0:T(1024)S(1)} fusion(s32[4096]{0:T(1024)S(1)} %compare_select_fusion.4, s32[4096]{0:T(1024)S(1)} %iota.177, s32[]{:T(128)} %constant.591.clone.1), kind=kCustom, calls=%fused_computation.334 | custom fusion | bytes 18436 | tf_op jit(solution)/shard_map/scatter | solution.py:65
  322.0 15.5 %scatter_custom_fusion.9 = s32[4608]{0:T(1024)S(1)} fusion(s32[4096]{0:T(1024)S(1)} %compare_select_fusion.1, s32[4096]{0:T(1024)S(1)} %iota.189, s32[]{:T(128)} %constant.591.clone.1), kind=kCustom, calls=%fused_computation.328 | custom fusion | bytes 18436 | tf_op jit(solution)/shard_map/scatter | solution.py:65
  341.1 44.3 %collective-permute-done.8 = bf16[2048,512]{1,0:T(8,128)(2,1)} collective-permute-done((bf16[2048,512]{1,0:T(8,128)(2,1)}, bf16[2048,512]{1,0:T(8,128)(2,1)}, u32[]{:S(2)}, u32[]{:S(2)}) %collective-permute-start.8) | collective-permute-done | bytes 2097184 | tf_op jit(solution)/shard_map/ppermute | solution.py:10
  490.4 11.7 cholesky.446
  514.6 11.7 cholesky.465
  537.9 11.7 cholesky.486
  595.2 39.3 %custom-call.30 = f32[4,128,128]{1,2,0:T(8,128)S(1)} custom-call(f32[4,128,128]{2,1,0:T(8,128)S(1)} %get-tuple-element.42), custom_call_target="InvertDiagBlocksLowerTriangular" | custom-call | tf_op jit(solution)/shard_map/triangular_solve | solution.py:166
  676.1 15.5 %scatter_custom_fusion.1 = s32[4608]{0:T(1024)S(1)} fusion(s32[4096]{0:T(1024)S(1)} %compare_select_fusion.5, s32[4096]{0:T(1024)S(1)} %iota.175, s32[]{:T(128)} %constant.591.clone.1), kind=kCustom, calls=%fused_computation.336 | custom fusion | bytes 18436 | tf_op jit(solution)/shard_map/scatter | solution.py:65
  692.3 15.5 %scatter_custom_fusion.11 = s32[4608]{0:T(1024)S(1)} fusion(s32[4096]{0:T(1024)S(1)} %compare_select_fusion, s32[4096]{0:T(1024)S(1)} %iota.197, s32[]{:T(128)} %constant.591.clone.1), kind=kCustom, calls=%fused_computation.326 | custom fusion | bytes 18436 | tf_op jit(solution)/shard_map/scatter | solution.py:65
  722.3 32.6 %collective-permute-done.19 = bf16[2048,512]{1,0:T(8,128)(2,1)} collective-permute-done((bf16[2048,512]{1,0:T(8,128)(2,1)}, bf16[2048,512]{1,0:T(8,128)(2,1)}, u32[]{:S(2)}, u32[]{:S(2)}) %collective-permute-start.19) | collective-permute-done | bytes 2097184 | tf_op jit(solution)/shard_map/ppermute | solution.py:10
  793.9 110.3 %all-gather.1 = f32[4,2,512]{2,1,0:T(2,128)S(1)} all-gather(f32[1,2,512]{2,1,0:T(2,128)S(1)} %slice_bitcast_fusion.25), channel_id=1, replica_groups=mesh['cube'=64,'panel'=4] {'panel'}, dimensions={0}, use_global_device_ids=true | all-gather | bytes 20480 | tf_op jit(solution)/shard_map/all_gather | solution.py:157
  1037.8 39.3 %custom-call.31 = f32[4,128,128]{1,2,0:T(8,128)S(1)} custom-call(f32[4,128,128]{2,1,0:T(8,128)S(1)} %get-tuple-element.50), custom_call_target="InvertDiagBlocksLowerTriangular" | custom-call | tf_op jit(solution)/shard_map/triangular_solve | solution.py:166
  1130.0 21.5 %collective-permute-done.31 = bf16[1024,512]{1,0:T(8,128)(2,1)S(1)} collective-permute-done((bf16[1024,512]{1,0:T(8,128)(2,1)S(1)}, bf16[1024,512]{1,0:T(8,128)(2,1)S(1)}, u32[]{:S(2)}, u32[]{:S(2)}) %collective-permute-start.31) | collective-permute-done | bytes 1048608 | tf_op jit(solution)/shard_map/ppermute | solution.py:10
  1153.3 43.6 %collective-permute-done.32 = bf16[2048,512]{1,0:T(8,128)(2,1)S(1)} collective-permute-done((bf16[2048,512]{1,0:T(8,128)(2,1)S(1)}, bf16[2048,512]{1,0:T(8,128)(2,1)S(1)}, u32[]{:S(2)}, u32[]{:S(2)}) %collective-permute-start.32) | collective-permute-done | bytes 2097184 | tf_op jit(solution)/shard_map/ppermute | solution.py:10
  (423 shorter events, 629.6 us)
Async XLA Ops:
  3.3 55.3 %collective-permute-start = (f32[64,4096]{1,0:T(8,128)}, f32[64,4096]{1,0:T(8,128)S(1)}, u32[]{:S(2)}, u32[]{:S(2)}) collective-permute-start(f32[64,4096]{1,0:T(8,128)} %get-tuple-element.97), channel_id=1, source_target_pairs={{0,32},{4,36},{8,40},{12,44},{16,48},{20,52},{24,56},{28,60},{32,0... | collective-permute-start | bytes 3145736 | tf_op jit(solution)/shard_map/ppermute | solution.py:10
  106.8 8.2 collective-permute-start.3
  115.0 11.6 collective-permute-start.4
  288.4 13.2 %collective-permute-start.6 = (bf16[512,512]{1,0:T(8,128)(2,1)S(1)}, bf16[512,512]{1,0:T(8,128)(2,1)S(1)}, u32[]{:S(2)}, u32[]{:S(2)}) collective-permute-start(bf16[512,512]{1,0:T(8,128)(2,1)S(1)} %maximum_select_fusion.16), channel_id=1, source_target_pairs={{0,8},{4,12},{8,0},{12,4},{16,24},{20,28},{24,16},{28,20},{32,40},... | collective-permute-start | bytes 1572872 | tf_op jit(solution)/shard_map/ppermute | solution.py:10
  302.1 35.5 %collective-permute-start.7 = (bf16[1024,512]{1,0:T(8,128)(2,1)S(1)}, bf16[1024,512]{1,0:T(8,128)(2,1)S(1)}, u32[]{:S(2)}, u32[]{:S(2)}) collective-permute-start(bf16[1024,512]{1,0:T(8,128)(2,1)S(1)} %maximum_select_fusion.10), channel_id=1, source_target_pairs={{0,16},{4,20},{8,24},{12,28},{16,0},{20,4},{24,8},{28,12},{32,48},... | collective-permute-start | bytes 3145736 | tf_op jit(solution)/shard_map/ppermute | solution.py:10
  339.5 46.0 %collective-permute-start.8 = (bf16[2048,512]{1,0:T(8,128)(2,1)}, bf16[2048,512]{1,0:T(8,128)(2,1)}, u32[]{:S(2)}, u32[]{:S(2)}) collective-permute-start(bf16[2048,512]{1,0:T(8,128)(2,1)} %maximum_select_fusion.6), channel_id=1, source_target_pairs={{0,32},{4,36},{8,40},{12,44},{16,48},{20,52},{24,56},{28,60},{32,0... | collective-permute-start | bytes 6291464 | tf_op jit(solution)/shard_map/ppermute | solution.py:10
  390.9 14.6 %collective-permute-start.9 = (f32[32,4096]{1,0:T(8,128)}, f32[32,4096]{1,0:T(8,128)S(1)}, u32[]{:S(2)}, u32[]{:S(2)}) collective-permute-start(f32[32,4096]{1,0:T(8,128)} %get-tuple-element.99), channel_id=1, source_target_pairs={{0,64},{4,68},{8,72},{12,76},{16,80},{20,84},{24,88},{28,92},{32,9... | collective-permute-start | bytes 1572872 | tf_op jit(solution)/shard_map/ppermute | solution.py:10
  438.7 7.6 collective-permute-start.11
  446.6 8.2 collective-permute-start.12
  460.8 27.8 %collective-permute-start.14 = (f32[256,512]{0,1:T(8,128)S(1)}, f32[256,512]{0,1:T(8,128)S(1)}, u32[]{:S(2)}, u32[]{:S(2)}) collective-permute-start(f32[256,512]{0,1:T(8,128)S(1)} %maximum_select_fusion.17), channel_id=1, source_target_pairs={{0,64},{4,68},{8,72},{12,76},{16,80},{20,84},{24,88},{28,92},{32,9... | collective-permute-start | bytes 1572872 | tf_op jit(solution)/shard_map/ppermute | solution.py:10
  463.2 86.4 %all-to-all-start = ((bf16[64,4,2,16]{3,2,1,0:T(2,128)(2,1)}), bf16[64,4,2,16]{3,2,1,0:T(2,128)(2,1)S(1)}, u32[]{:S(2)}, u32[]{:S(2)}) async-start(bf16[64,4,2,16]{3,2,1,0:T(2,128)(2,1)} %bitcast.45), calls=%async_computation | async-start | bytes 262144 | tf_op jit(solution)/shard_map/all_to_all | solution.py:38
  549.7 163.1 %all-to-all-start.2 = ((bf16[64,4,2,4608]{3,2,1,0:T(2,128)(2,1)}), bf16[64,4,2,4608]{3,2,1,0:T(2,128)(2,1)}, u32[]{:S(2)}, u32[]{:S(2)}) async-start(bf16[64,4,2,4608]{3,2,1,0:T(2,128)(2,1)} %reshape.273), calls=%async_computation.2 | async-start | bytes 9437184 | tf_op jit(solution)/shard_map/all_to_all | solution.py:31
  659.3 14.2 %collective-permute-start.17 = (bf16[512,512]{1,0:T(8,128)(2,1)S(1)}, bf16[512,512]{1,0:T(8,128)(2,1)S(1)}, u32[]{:S(2)}, u32[]{:S(2)}) collective-permute-start(bf16[512,512]{1,0:T(8,128)(2,1)S(1)} %maximum_select_fusion.18), channel_id=1, source_target_pairs={{0,16},{4,20},{8,24},{12,28},{16,0},{20,4},{24,8},{28,12},{32,48},... | collective-permute-start | bytes 1572872 | tf_op jit(solution)/shard_map/ppermute | solution.py:10
  673.9 34.0 %collective-permute-start.18 = (bf16[1024,512]{1,0:T(8,128)(2,1)S(1)}, bf16[1024,512]{1,0:T(8,128)(2,1)S(1)}, u32[]{:S(2)}, u32[]{:S(2)}) collective-permute-start(bf16[1024,512]{1,0:T(8,128)(2,1)S(1)} %maximum_select_fusion.12), channel_id=1, source_target_pairs={{0,32},{4,36},{8,40},{12,44},{16,48},{20,52},{24,56},{28,60},{32,0... | collective-permute-start | bytes 3145736 | tf_op jit(solution)/shard_map/ppermute | solution.py:10
  709.8 45.0 %collective-permute-start.19 = (bf16[2048,512]{1,0:T(8,128)(2,1)}, bf16[2048,512]{1,0:T(8,128)(2,1)}, u32[]{:S(2)}, u32[]{:S(2)}) collective-permute-start(bf16[2048,512]{1,0:T(8,128)(2,1)} %maximum_select_fusion.7), channel_id=1, source_target_pairs={{0,64},{4,68},{8,72},{12,76},{16,80},{20,84},{24,88},{28,92},{32,9... | collective-permute-start | bytes 6291464 | tf_op jit(solution)/shard_map/ppermute | solution.py:10
  712.7 76.1 %all-to-all-start.1 = ((bf16[4,2,1024]{2,1,0:T(2,128)(2,1)}), bf16[4,2,1024]{2,1,0:T(2,128)(2,1)S(1)}, u32[]{:S(2)}, u32[]{:S(2)}) async-start(bf16[4,2,1024]{2,1,0:T(2,128)(2,1)} %reshape.834), calls=%async_computation.1 | async-start | bytes 32768 | tf_op jit(solution)/shard_map/all_to_all | solution.py:37
  759.5 16.0 %collective-permute-start.20 = (f32[16,4096]{1,0:T(8,128)S(1)}, f32[16,4096]{1,0:T(8,128)S(1)}, u32[]{:S(2)}, u32[]{:S(2)}) collective-permute-start(f32[16,4096]{1,0:T(8,128)S(1)} %get-tuple-element.101), channel_id=1, source_target_pairs={{0,128},{4,132},{8,136},{12,140},{16,144},{20,148},{24,152},{28,15... | collective-permute-start | bytes 786440 | tf_op jit(solution)/shard_map/ppermute | solution.py:10
  788.9 288.3 %all-to-all-start.3 = ((bf16[64,4,2,4608]{3,0,2,1:T(8,128)(2,1)}), bf16[64,4,2,4608]{3,0,2,1:T(8,128)(2,1)}, u32[]{:S(2)}, u32[]{:S(2)}) async-start(bf16[64,4,2,4608]{3,0,2,1:T(8,128)(2,1)} %copy.76), calls=%async_computation.3 | async-start | bytes 9437184 | tf_op jit(solution)/shard_map/all_to_all | solution.py:30
  925.8 10.4 collective-permute-start.26
  1093.8 10.7 collective-permute-start.27
  1109.5 8.2 collective-permute-start.29
  1117.9 11.4 collective-permute-start.30
  1129.8 21.7 %collective-permute-start.31 = (bf16[1024,512]{1,0:T(8,128)(2,1)S(1)}, bf16[1024,512]{1,0:T(8,128)(2,1)S(1)}, u32[]{:S(2)}, u32[]{:S(2)}) collective-permute-start(bf16[1024,512]{1,0:T(8,128)(2,1)S(1)} %maximum_select_fusion.14), channel_id=1, source_target_pairs={{0,64},{4,68},{8,72},{12,76},{16,80},{20,84},{24,88},{28,92},{32,9... | collective-permute-start | bytes 3145736 | tf_op jit(solution)/shard_map/ppermute | solution.py:10
  1152.2 44.8 %collective-permute-start.32 = (bf16[2048,512]{1,0:T(8,128)(2,1)S(1)}, bf16[2048,512]{1,0:T(8,128)(2,1)S(1)}, u32[]{:S(2)}, u32[]{:S(2)}) collective-permute-start(bf16[2048,512]{1,0:T(8,128)(2,1)S(1)} %maximum_select_fusion.8), channel_id=1, source_target_pairs={{0,128},{4,132},{8,136},{12,140},{16,144},{20,148},{24,152},{28,15... | collective-permute-start | bytes 6291464 | tf_op jit(solution)/shard_map/ppermute | solution.py:10
  (26 other events, 558.7 us)
where the time goes:
time: 1210 us; the launch traced here: 1200 us
  other arithmetic  379 us (31%)
  waiting for transfers between devices  260 us (21%)
  local copies, waits for them, and re-layouts  245 us (20%)
  blocking collectives  169 us (14%)
  starting transfers between devices  96.6 us (8%)
  matrix products  38.3 us (3%)
    ppermute x33, waiting for transfers between devices, from_partner(): lax.ppermute(shard, axis, [(i, i ^ 1 << stride) for i in range(lax.axis_s...  260 us
    another operation x45, other arithmetic, body(): chol_lower = jnp.linalg.cholesky(pivot_block)  238 us
    all_gather x3, blocking collectives, body(): pivot_block = lax.all_gather(pivot_rows, 'panel', axis=0, tiled=True)  135 us
    another operation x10, other arithmetic, body(): lax.linalg.triangular_solve(chol_lower, coupled, left_side=False, lower=T...  119 us
    scatter x6, local copies, waits for them, and re-layouts, place_rows(): columns = jnp.full((order_full,), -1, jnp.int32).at[child_map].set(jnp.ar...  93.2 us
    gather x12, local copies, waits for them, and re-layouts, place_rows(): picked = jnp.take(picked, jnp.maximum(columns, 0), axis=1)  71 us
    ppermute x33, starting transfers between devices, from_partner(): lax.ppermute(shard, axis, [(i, i ^ 1 << stride) for i in range(lax.axis_s...  69.1 us
    all_gather x3, blocking collectives, body(): collected = lax.all_gather(factor, 'panel', axis=0, tiled=True)  34.2 us
  transfers between devices with their start and end apart: 37, of which 27 were waited for; matrix products, arithmetic and copies ran while one was open for 39% of the time, Pallas kernels for 0%

commit v1 on v0

v1 whole, which is shorter than its diff:
```python
import functools
import jax
import jax.numpy as jnp
from jax import lax
from jax.experimental import pallas as pl
from jax.experimental.pallas import tpu as pltpu
from jax.sharding import PartitionSpec as P

CAP = 2
K = 512
U = 4096
PANELS = 4
f32, bf16, i32 = jnp.float32, jnp.bfloat16, jnp.int32
VMEM = pl.BlockSpec(memory_space=pltpu.VMEM)


def split(x):
    hi = x.astype(bf16)
    return hi, (x - hi.astype(f32)).astype(bf16)

def mm(x, y, dims):
    xh, xl = split(x); yh, yl = split(y)
    d = functools.partial(lax.dot_general, dimension_numbers=(dims, ((), ())), preferred_element_type=f32)
    return d(xh, yh) + (d(xh, yl) + d(xl, yh))

def diag_inverse(V, ahead=2):
    V = list(V)
    lane = lax.broadcasted_iota(jnp.int32, (8, 128), 1)
    sub = lax.broadcasted_iota(jnp.int32, (8, 128), 0)
    below = [sub > i for i in range(8)]
    scale = []
    for g in range(8):
        p0, j0 = 2 * g, 16 * g
        win = [q for q in range(p0, min(p0 + 2 + ahead, 16))]
        B = {(k, q): jnp.broadcast_to(V[q][:, j0+k:j0+k+1], (8, 128)) for k in range(16) for q in win}
        dinv = [None, None]
        for i in range(16):
            s, ii = divmod(i, 8)
            ps = p0 + s
            j = j0 + i
            inv = 1.0 / jnp.broadcast_to(B[i, ps][ii:ii+1, :], (8, 128))
            dinv[s] = inv if ii == 0 else jnp.where(below[ii-1], inv, dinv[s])
            at = lane == j
            row = jnp.where(at, 1.0, jnp.broadcast_to(V[ps][ii:ii+1, :], (8, 128)))
            splats = {k: jnp.broadcast_to(B[k, ps][ii:ii+1, :], (8, 128)) for k in range(i+1, 16)}
            for q in win:
                if q < ps or (q == ps and ii == 7): continue
                m = B[i, q] * inv
                if q == ps:
                    m = jnp.where(below[ii], m, 0.0)
                    z = jnp.where(at & below[ii], 0.0, V[q])
                else:
                    z = jnp.where(at, 0.0, V[q])
                V[q] = z - m * row
                for k in range(i+1, 16):
                    B[k, q] = B[k, q] - m * splats[k]
        scale += dinv
        rest = range(p0 + 2 + ahead, 16)
        if len(rest):
            G, Q = [], []
            for s in range(2):
                r = sub + (j0 + 8 * s)
                v = V[p0 + s]
                Q.append(v * dinv[s])
                inwin = (lane >= j0) & (lane < j0 + 16)
                G.append(jnp.where(inwin, jnp.where(lane < r, v, jnp.where(lane == r, 1.0, 0.0)), v))
            Gc, Qc = jnp.concatenate(G, 0), jnp.concatenate(Q, 0)
            gh, gl = split(Gc); qh, ql = split(Qc)
            upd = lax.dot_general(jnp.concatenate([qh, qh, ql], 0), jnp.concatenate([gh, gl, gh], 0),
                                  (((0,), (0,)), ((), ())), preferred_element_type=f32)
            zw = (lane >= j0) & (lane < j0 + 16)
            for q in rest:
                V[q] = jnp.where(zw, 0.0, V[q]) - upd[8*q:8*q+8]
    out = []
    for p in range(16):
        r = sub + 8 * p
        s = jnp.sqrt(scale[p])
        out.append(jnp.where(lane < r, V[p] * s, jnp.where(lane == r, s, 0.0)))
    return out


def place(level):
    group = 16 << level
    cube_at = lax.axis_index("cube")
    position = lax.rem(cube_at, group)
    return group, position, cube_at // group, position // (group // 2)


def assemble_kernel(level, *refs):
    maps, diag, mine, other = refs[:4]
    extra = refs[4] if level == 2 else None
    piv_out, coupled_out, upd_out, map_row, diag_row = refs[-5:]
    group, position, front_at, side = place(level)
    panel_at = lax.axis_index("panel")
    r = U // (group * PANELS)
    k = K // (group * PANELS)
    map_base = (0, 8, 12)[level]
    diag_base = (0, 4, 6)[level]
    block = lax.rem(position, group // 2) * PANELS + panel_at
    parent = position * PANELS + panel_at
    map_row[0:1, :] = maps[pl.ds(map_base + 2 * front_at + side, 1), :]
    map_row[1:2, :] = maps[pl.ds(map_base + 2 * front_at + 1 - side, 1), :]
    diag_row[0:1, :] = diag[pl.ds(diag_base + front_at, 1), :]
    lane = lax.broadcasted_iota(i32, (1, 128), 1)
    height = 16 + r

    def row_choice(half):
        start = block * (2 * r)
        tile = map_row[half:half + 1, pl.ds(pl.multiple_of(start // 128 * 128, 128), 128)]
        shift = lax.rem(128 - lax.rem(start + half * r, 128), 128)
        t = pltpu.roll(jnp.broadcast_to(tile, (8, 128)), shift, 1)[:1, :r]
        slot = jnp.where(t < K, t - parent * k, 16 + t - K - parent * r)
        rows = lax.broadcasted_iota(i32, (height, r), 0)
        return (rows == slot).astype(f32).astype(bf16)

    sel = (row_choice(0), row_choice(1))
    sides = (side, 1 - side)
    spread = lax.broadcasted_iota(i32, (128, 256), 0)
    piv_acc = [None, None]
    out_rows = lax.broadcasted_iota(i32, (height, 128), 0)
    upd_row_id = parent * r + out_rows - 16
    piv_row_id = parent * k + out_rows
    for c in range(16):
        xs, ss = [], []
        for which, ref in enumerate((mine, other)):
            x = ref[:, c * 256:(c + 1) * 256]
            hi, lo = split(x)
            pick = lambda y: jnp.dot(sel[which], y, preferred_element_type=f32).astype(bf16)
            xs.append(jnp.concatenate([pick(hi), pick(lo)], axis=0))
            m = map_row[which:which + 1, c * 256:(c + 1) * 256]
            onehots = [
                spread == m - (K + s * (U // 2) + c * 128) for s in sides
            ] + [spread == m - (s * (K // 2) + c // 8 * 128) for s in sides]
            ss.append(jnp.concatenate([o.astype(f32).astype(bf16) for o in onehots], axis=0))
        res = lax.dot_general(
            jnp.concatenate(xs, axis=1), jnp.concatenate(ss, axis=1),
            (((1,), (1,)), ((), ())), preferred_element_type=f32,
        )
        res = res[:height] + res[height:]
        upd_col = side * (U // 2) + c * 128 + lane
        d = diag_row[0:1, pl.ds(pl.multiple_of(K + side * (U // 2) + c * 128, 128), 128)]
        own = res[:, :128] + jnp.where(upd_row_id == upd_col, d, 0.0)
        for at, tile in ((side, own), (1 - side, res[:, 128:256])):
            cols = pl.ds(pl.multiple_of(at * (U // 2) + c * 128, 128), 128)
            value = tile[16:]
            if extra is not None:
                value += extra[:, pl.ds(pl.multiple_of(K + at * (U // 2) + c * 128, 128), 128)]
            upd_out[:, cols] = value
        for n in range(2):
            part = res[:, 256 + n * 128:384 + n * 128]
            piv_acc[n] = part if c % 8 == 0 else piv_acc[n] + part
        if c % 8 == 7:
            half = c // 8
            col = side * (K // 2) + half * 128 + lane
            d = diag_row[0:1, pl.ds(pl.multiple_of(side * (K // 2) + half * 128, 128), 128)]
            piv_acc[0] += jnp.where((piv_row_id == col) & (out_rows < 16), d, 0.0)
            for n, at in enumerate((side, 1 - side)):
                cols = pl.ds(pl.multiple_of(at * (K // 2) + half * 128, 128), 128)
                value = piv_acc[n][16:]
                if extra is not None:
                    value += extra[:, cols]
                coupled_out[:, cols] = value
                piv_out[pl.ds(2 * at + half, k, stride=4), :] = piv_acc[n][:k]


def assemble(level, maps, diag, mine, other, extra):
    r = mine.shape[0]
    k = r // 8
    ins = (maps, diag, mine, other) + ((extra,) if level == 2 else ())
    return pl.pallas_call(
        functools.partial(assemble_kernel, level),
        out_shape=(
            jax.ShapeDtypeStruct((4 * k, 128), f32),
            jax.ShapeDtypeStruct((r, K), f32),
            jax.ShapeDtypeStruct((r, U), f32),
        ),
        in_specs=[VMEM] * len(ins),
        out_specs=(VMEM,) * 3,
        scratch_shapes=[pltpu.VMEM((8, U), i32), pltpu.VMEM((8, U + K), f32)],
        compiler_params=pltpu.CompilerParams(vmem_limit_bytes=40 * 2**20),
        name="assemble%d" % level,
    )(*ins)


def factor_kernel(level, *refs):
    pivots, coupled = refs[:2]
    out, w = refs[-2:]
    r = coupled.shape[0]
    n = K
    ct = coupled[...]
    if level == 2:
        order = refs[2]
        move = (lax.broadcasted_iota(i32, (n, n), 0) == order[...]).astype(f32).astype(bf16)
        ch, cl = split(ct)
        ct = jnp.dot(ch, move, preferred_element_type=f32) + jnp.dot(cl, move, preferred_element_type=f32)
        a = jnp.concatenate([pivots[pl.ds(c, n, stride=4), :] for c in range(4)], axis=1)
        ah, al = split(a)
        for part, source in enumerate((ah, al)):
            cols = jnp.dot(source, move, preferred_element_type=f32).astype(bf16)
            both = lax.dot_general(move, cols, (((0,), (0,)), ((), ())), preferred_element_type=f32)
            if part == 0:
                w[:, :n] = both
            else:
                w[:, :n] += both
    else:
        for c in range(4):
            w[:, c * 128:(c + 1) * 128] = pivots[pl.ds(c, n, stride=4), :]
    if r < 128:
        ct = jnp.concatenate([ct, jnp.zeros((128 - r, n), f32)], axis=0)
    w[:, n:] = ct.T
    blocks = n // 128
    for b in range(blocks):
        lo = b * 128
        rows = [w[lo + 8 * p: lo + 8 * p + 8, lo:lo + 128] for p in range(16)]
        inverse = jnp.concatenate(diag_inverse(rows), axis=0)
        solved = mm(inverse, w[lo:lo + 128, lo + 128:], ((1,), (0,)))
        for later in range(b + 1, blocks):
            off = (later - b - 1) * 128
            w[later * 128:(later + 1) * 128, later * 128:] -= mm(
                solved[:, off:off + 128], solved[:, off:], ((0,), (0,))
            )
        out[:, lo:lo + 128] = solved[:, n - lo - 128:].T[:r].astype(bf16)


def make_factor(level, pivots, coupled, order):
    r = coupled.shape[0]
    ins = (pivots, coupled) + ((order,) if level == 2 else ())
    return pl.pallas_call(
        functools.partial(factor_kernel, level),
        out_shape=jax.ShapeDtypeStruct((r, K), bf16),
        in_specs=[VMEM] * len(ins),
        out_specs=VMEM,
        scratch_shapes=[pltpu.VMEM((K, K + 128), f32)],
        compiler_params=pltpu.CompilerParams(vmem_limit_bytes=32 * 2**20),
        name="factor%d" % level,
    )(*ins)


def gather_kernel(ysize, x_ref, out, send_sem, recv_sem, local_sem):
    cube_at = lax.axis_index("cube")
    zh = lax.axis_index("panel")
    core = lax.rem(cube_at, 2)
    x = lax.rem(cube_at // 2, 4)
    zl = lax.rem(cube_at // 8, 2)
    yfull = cube_at // 16
    y = lax.rem(yfull, ysize)
    ybase = yfull - y

    def target(y, zl, x, core, zh):
        return {"cube": (ybase + y) * 16 + zl * 8 + x * 2 + core, "panel": zh}

    def shifted(v, d, size):
        return lax.rem(v + d, size)

    z_peers = [
        target(y, shifted(zl, a, 2), x, core, shifted(zh, b, 4))
        for a in range(2) for b in range(4) if a + b
    ]
    x_peers = [target(y, zl, shifted(x, d, 4), core, zh) for d in range(1, 4)]
    y_peers = [target(shifted(y, d, ysize), zl, x, core, zh) for d in range(1, ysize)]
    core_peers = [target(y, zl, x, 1 - core, zh)]
    stages = [
        (z_peers, out.at[y, zl, x, core, zh]),
        (x_peers, out.at[y, :, x, core]),
        (y_peers, out.at[y, :, :, core]),
        (core_peers, out.at[:, :, :, core]),
    ]
    everyone = z_peers + x_peers + y_peers + core_peers
    keep = pltpu.make_async_copy(x_ref, out.at[y, zl, x, core, zh], local_sem)
    keep.start()
    barrier = pltpu.get_barrier_semaphore()
    for peer in everyone:
        pl.semaphore_signal(barrier, inc=1, device_id=peer, device_id_type=pl.DeviceIdType.MESH)
    pl.semaphore_wait(barrier, len(everyone))
    keep.wait()
    number = 0
    sent = []
    for peers, part in stages:
        copies = []
        for peer in peers:
            copies.append(pltpu.make_async_remote_copy(
                src_ref=part, dst_ref=part, send_sem=send_sem.at[number], recv_sem=recv_sem.at[number],
                device_id=peer, device_id_type=pl.DeviceIdType.MESH,
            ))
            number += 1
        for copy in copies:
            copy.start()
        for copy in copies:
            copy.wait_recv()
        sent += copies
    for copy in sent:
        copy.wait_send()


def gather(level, piece, ident):
    ysize = 1 << level
    rows, cols = piece.shape
    count = 7 + 3 + ysize - 1 + 1
    out = pl.pallas_call(
        functools.partial(gather_kernel, ysize),
        out_shape=jax.ShapeDtypeStruct((ysize, 2, 4, 2, 4, rows, cols), piece.dtype),
        in_specs=[VMEM],
        out_specs=VMEM,
        scratch_shapes=[
            pltpu.SemaphoreType.DMA((count,)), pltpu.SemaphoreType.DMA((count,)),
            pltpu.SemaphoreType.DMA(()),
        ],
        compiler_params=pltpu.CompilerParams(
            collective_id=ident, has_side_effects=True, vmem_limit_bytes=32 * 2**20
        ),
        name="gather%d" % ident,
    )(piece)
    return out.reshape(-1, cols)


def from_partner(shard, stride):
    return lax.ppermute(shard, "cube", [(i, i ^ 1 << stride) for i in range(64)])


def route_rows(coupling_rows, coupling_owner, coupling_slot):
    cubes, panels, root_rows = 64, PANELS, 16
    owners = coupling_owner[:, 0]
    owner_count = cubes * panels
    owner_hits = (owners[:, None] == jnp.arange(owner_count, dtype=i32)[None, :]).astype(i32)
    earlier = jnp.sum((jnp.cumsum(owner_hits, axis=0) - owner_hits) * owner_hits, axis=1)
    target = owners * CAP + earlier
    row_width = coupling_rows.shape[1]
    choose = (target[None, :] == jnp.arange(owner_count * CAP, dtype=i32)[:, None]).astype(bf16)
    marks = (coupling_slot[:, None] == jnp.arange(root_rows, dtype=i32)[None, :]).astype(bf16)
    outgoing = jnp.dot(choose, coupling_rows, preferred_element_type=f32).astype(bf16)
    labels = jnp.dot(choose, marks, preferred_element_type=f32).astype(bf16)
    outgoing = outgoing.reshape(cubes, panels, CAP, row_width)
    labels = labels.reshape(cubes, panels, CAP, root_rows)

    def spread(v):
        v = lax.all_to_all(v, "cube", split_axis=0, concat_axis=0, tiled=True)
        return lax.all_to_all(v, "panel", split_axis=1, concat_axis=1, tiled=True)

    return jnp.einsum("abcr,abcf->rf", spread(labels), spread(outgoing), preferred_element_type=f32)


def body(leaf_updates, extend_maps, front_diagonal, pivot_order, coupling_rows, coupling_owner, coupling_slot):
    assembly = route_rows(coupling_rows, coupling_owner, coupling_slot)
    children = leaf_updates
    order = pivot_order.reshape(1, K)
    for level in range(3):
        r = children.shape[0] // 2
        incoming = from_partner(children[r:], 3 + level)
        piece, coupled, update_rows = assemble(
            level, extend_maps, front_diagonal, children[:r], incoming, assembly
        )
        pivots = gather(level, piece, 2 * level)
        factor = make_factor(level, pivots, coupled, order)
        collected = gather(level, factor, 2 * level + 1)
        product = lax.dot_general(
            factor, collected, (((1,), (1,)), ((), ())), preferred_element_type=f32
        )
        children = update_rows - product
    return (factor, children)


def solution(mesh):
    return jax.shard_map(
        body,
        mesh=mesh,
        in_specs=(
            P(("cube", "panel"), None), P(), P(), P(),
            P(("cube", "panel"), None), P(("cube", "panel"), None), P(("cube", "panel")),
        ),
        out_specs=(P(("cube", "panel"), None), P(("cube", "panel"), None)),
        check_vma=False,
    )
```

time: 1210 us -> 539 us (0.45)
  other arithmetic: 379 us -> 2.74 us
  Pallas kernels: 0 us -> 259 us
  local copies, waits for them, and re-layouts: 245 us -> 20.1 us
  blocking collectives: 169 us -> 0 us
  waiting for transfers between devices: 260 us -> 200 us
  starting transfers between devices: 96.6 us -> 37.1 us
  matrix products: 38.3 us -> 11.5 us
    another operation x58 -> x3, other arithmetic: 357 us -> 0.26 us  [the longest x45 238 us: body(): chol_lower = jnp.linalg.cholesky(pivot_block)]
    pallas_call x0 -> x12, Pallas kernels: none -> 259 us  [the longest x6 205 us: gather(): pl.pallas_call(functools.partial(gather_kernel, ysize), out_shape=jax.Sha...]
    all_gather x6 -> x0, blocking collectives: 169 us -> none  [the longest x3 135 us: body(): pivot_block = lax.all_gather(pivot_rows, 'panel', axis=0, tiled=True)]
    ppermute x33 -> x3, waiting for transfers between devices: 260 us -> 140 us  [from_partner(): lax.ppermute(shard, 'cube', [(i, i ^ 1 << stride) for i in range(64)])]
    scatter x13 -> x0, local copies, waits for them, and re-layouts: 105 us -> none  [the longest x6 93.2 us: place_rows(): columns = jnp.full((order_full,), -1, jnp.int32).at[child_map].set(jnp.ar...]
    gather x25 -> x0, local copies, waits for them, and re-layouts: 83.8 us -> none  [the longest x12 71 us: place_rows(): picked = jnp.take(picked, jnp.maximum(columns, 0), axis=1)]
    ppermute x33 -> x3, starting transfers between devices: 69.1 us -> 4.79 us  [from_partner(): lax.ppermute(shard, 'cube', [(i, i ^ 1 << stride) for i in range(64)])]
    all_to_all x4, waiting for transfers between devices: 0.01 us -> 60.1 us  [the longest x2 59.1 us: spread(): v = lax.all_to_all(v, 'cube', split_axis=0, concat_axis=0, tiled=True)]
  transfers between devices with their start and end apart: 37 -> 7, of which waited for: 27 -> 5; matrix products, arithmetic and copies ran while one was open for 39% -> 5% of each run, Pallas kernels for 0% -> 32%
where the time goes in v1:
time: 539 us; the launch traced here: 531 us
  Pallas kernels  259 us (48%)
  waiting for transfers between devices  200 us (37%)
  starting transfers between devices  37.1 us (7%)
  local copies, waits for them, and re-layouts  20.1 us (4%)
  matrix products  11.5 us (2%)
    pallas_call x6, Pallas kernels, gather(): pl.pallas_call(functools.partial(gather_kernel, ysize), out_shape=jax.Sha...  205 us
    ppermute x3, waiting for transfers between devices, from_partner(): lax.ppermute(shard, 'cube', [(i, i ^ 1 << stride) for i in range(64)])  140 us
    all_to_all x2, waiting for transfers between devices, spread(): v = lax.all_to_all(v, 'cube', split_axis=0, concat_axis=0, tiled=True)  59.1 us
    pallas_call x3, Pallas kernels, make_factor(): pl.pallas_call(functools.partial(factor_kernel, level), out_shape=jax.Sha...  40.8 us
    all_to_all x2, starting transfers between devices, spread(): v = lax.all_to_all(v, 'cube', split_axis=0, concat_axis=0, tiled=True)  19.4 us
    pallas_call x3, Pallas kernels, assemble(): pl.pallas_call(functools.partial(assemble_kernel, level), out_shape=(jax....  13.2 us
    all_to_all x2, starting transfers between devices, spread(): return lax.all_to_all(v, 'panel', split_axis=1, concat_axis=1, tiled=True)  12.9 us
  transfers between devices with their start and end apart: 7, of which 5 were waited for; matrix products, arithmetic and copies ran while one was open for 5% of the time, Pallas kernels for 32%

profile of v1, /device:TPU:1, one launch (start us, length us, event | category | flops | bytes accessed | tf_op | source)
XLA Modules:
  0.0 531.4 jit_solution(9097265006328260238)
XLA Ops:
  5.2 10.3 %all-to-all-start = ((bf16[64,4,2,16]{3,2,1,0:T(2,128)(2,1)}), bf16[64,4,2,16]{3,2,1,0:T(2,128)(2,1)S(1)}, u32[]{:S(2)}, u32[]{:S(2)}) async-start(bf16[64,4,2,16]{3,2,1,0:T(2,128)(2,1)} %bitcast.9), calls=%async_computation | async-start | bytes 262144 | tf_op jit(solution)/shard_map/all_to_all | solution.py:336
  15.5 3.6 convolution_convert_fusion
  19.1 7.5 %reshape.62 = bf16[64,4,2,4608]{3,2,1,0:T(2,128)(2,1)} reshape(bf16[512,4608]{1,0:T(8,128)(2,1)} %convolution_convert_fusion) | data formatting | bytes 9437184 | tf_op jit(solution)/shard_map/reshape | solution.py:332
  26.6 9.0 %all-to-all-start.2 = ((bf16[64,4,2,4608]{3,2,1,0:T(2,128)(2,1)}), bf16[64,4,2,4608]{3,2,1,0:T(2,128)(2,1)}, u32[]{:S(2)}, u32[]{:S(2)}) async-start(bf16[64,4,2,4608]{3,2,1,0:T(2,128)(2,1)} %reshape.62), calls=%async_computation.2 | async-start | bytes 9437184 | tf_op jit(solution)/shard_map/all_to_all | solution.py:336
  36.5 59.1 %all-to-all-done.2 = bf16[64,4,2,4608]{3,2,1,0:T(2,128)(2,1)} async-done(((bf16[64,4,2,4608]{3,2,1,0:T(2,128)(2,1)}), bf16[64,4,2,4608]{3,2,1,0:T(2,128)(2,1)}, u32[]{:S(2)}, u32[]{:S(2)}) %all-to-all-start.2) | async-done | bytes 4718624 | tf_op jit(solution)/shard_map/all_to_all | solution.py:336
  95.6 7.3 %all-to-all-start.1 = ((bf16[4,2,1024]{2,1,0:T(2,128)(2,1)}), bf16[4,2,1024]{2,1,0:T(2,128)(2,1)S(1)}, u32[]{:S(2)}, u32[]{:S(2)}) async-start(bf16[4,2,1024]{2,1,0:T(2,128)(2,1)} %reshape.67), calls=%async_computation.1 | async-start | bytes 32768 | tf_op jit(solution)/shard_map/all_to_all | solution.py:337
  102.9 5.8 %copy.21 = bf16[64,4,2,4608]{3,0,2,1:T(8,128)(2,1)} copy(bf16[64,4,2,4608]{3,2,1,0:T(2,128)(2,1)} %all-to-all-done.2) | data formatting | bytes 9437184 | tf_op jit(solution)/shard_map/all_to_all | solution.py:336
  109.7 5.7 %all-to-all-start.3 = ((bf16[64,4,2,4608]{3,0,2,1:T(8,128)(2,1)}), bf16[64,4,2,4608]{3,0,2,1:T(8,128)(2,1)}, u32[]{:S(2)}, u32[]{:S(2)}) async-start(bf16[64,4,2,4608]{3,0,2,1:T(8,128)(2,1)} %copy.21), calls=%async_computation.3 | async-start | bytes 9437184 | tf_op jit(solution)/shard_map/all_to_all | solution.py:337
  118.0 122.2 %collective-permute-done.refs_3_ = f32[64,4096]{1,0:T(8,128)S(1)} collective-permute-done((f32[64,4096]{1,0:T(8,128)S(1)}, f32[64,4096]{1,0:T(8,128)S(1)}, u32[]{:S(2)}, u32[]{:S(2)}) %collective-permute-start) | collective-permute-done | bytes 1048608 | tf_op jit(solution)/shard_map/ppermute | solution.py:317
  240.2 4.4 assemble0.1
  244.6 19.7 %gather0.1 = f32[1,2,4,2,4,32,128]{6,5,4,3,2,1,0:T(8,128)S(1)} custom-call(f32[32,128]{1,0:T(8,128)S(1)} %get-tuple-element.12.x_ref), custom_call_target="tpu_custom_call" | custom-call | tf_op jit(solution)/shard_map/gather0/pallas_call | solution.py:299
  264.2 12.9 %factor0.1.x_ref = bf16[64,512]{1,0:T(8,128)(2,1)S(1)} custom-call(f32[2048,128]{1,0:T(8,128)S(1)} %bitcast.42, f32[64,512]{1,0:T(8,128)S(1)} %get-tuple-element.13.refs_1_), custom_call_target="tpu_custom_call" | custom-call | tf_op jit(solution)/shard_map/factor0/pallas_call | solution.py:228
  277.1 46.4 %gather1.1 = bf16[1,2,4,2,4,64,512]{6,5,4,3,2,1,0:T(8,128)(2,1)S(1)} custom-call(bf16[64,512]{1,0:T(8,128)(2,1)S(1)} %factor0.1.x_ref), custom_call_target="tpu_custom_call" | custom-call | tf_op jit(solution)/shard_map/gather1/pallas_call | solution.py:299
  329.0 12.4 %collective-permute-done.1.refs_3_ = f32[32,4096]{1,0:T(8,128)} collective-permute-done((f32[32,4096]{1,0:T(8,128)}, f32[32,4096]{1,0:T(8,128)}, u32[]{:S(2)}, u32[]{:S(2)}) %collective-permute-start.1) | collective-permute-done | bytes 524320 | tf_op jit(solution)/shard_map/ppermute | solution.py:317
  341.4 5.1 assemble1.1
  346.5 21.3 %gather2.1 = f32[2,2,4,2,4,16,128]{6,5,4,3,2,1,0:T(8,128)S(1)} custom-call(f32[16,128]{1,0:T(8,128)S(1)} %get-tuple-element.15.x_ref), custom_call_target="tpu_custom_call" | custom-call | tf_op jit(solution)/shard_map/gather2/pallas_call | solution.py:299
  367.8 12.9 %factor1.1.x_ref = bf16[32,512]{1,0:T(8,128)(2,1)S(1)} custom-call(f32[2048,128]{1,0:T(8,128)S(1)} %bitcast.43, f32[32,512]{1,0:T(8,128)S(1)} %get-tuple-element.16.refs_1_), custom_call_target="tpu_custom_call" | custom-call | tf_op jit(solution)/shard_map/factor1/pallas_call | solution.py:228
  380.7 49.8 %gather3.1 = bf16[2,2,4,2,4,32,512]{6,5,4,3,2,1,0:T(8,128)(2,1)S(1)} custom-call(bf16[32,512]{1,0:T(8,128)(2,1)S(1)} %factor1.1.x_ref), custom_call_target="tpu_custom_call" | custom-call | tf_op jit(solution)/shard_map/gather3/pallas_call | solution.py:299
  433.5 3.1 convolution_bitcast_fusion.refs_4_
  436.6 5.6 %collective-permute-done.2.refs_3_ = f32[16,4096]{1,0:T(8,128)S(1)} collective-permute-done((f32[16,4096]{1,0:T(8,128)}, f32[16,4096]{1,0:T(8,128)S(1)}, u32[]{:S(2)}, u32[]{:S(2)}) %collective-permute-start.2) | collective-permute-done | bytes 262176 | tf_op jit(solution)/shard_map/ppermute | solution.py:317
  442.3 3.8 assemble2.1
  446.0 22.7 %gather4.1 = f32[4,2,4,2,4,8,128]{6,5,4,3,2,1,0:T(8,128)S(1)} custom-call(f32[8,128]{1,0:T(8,128)S(1)} %get-tuple-element.17.x_ref), custom_call_target="tpu_custom_call" | custom-call | tf_op jit(solution)/shard_map/gather4/pallas_call | solution.py:299
  468.8 15.0 %factor2.1.x_ref = bf16[16,512]{1,0:T(8,128)(2,1)} custom-call(f32[2048,128]{1,0:T(8,128)S(1)} %bitcast.44, f32[16,512]{1,0:T(8,128)S(1)} %get-tuple-element.18.refs_1_, s32[1,512]{1,0:T(1,128)S(1)} %bitcast.45), custom_call_target="tpu_custom_call" | custom-call | tf_op jit(solution)/shard_map/factor2/pallas_call | solution.py:228
  484.5 44.7 %gather5.1 = bf16[4,2,4,2,4,16,512]{6,5,4,3,2,1,0:T(8,128)(2,1)S(1)} custom-call(bf16[16,512]{1,0:T(8,128)(2,1)S(1)} %copy-done.3), custom_call_target="tpu_custom_call" | custom-call | tf_op jit(solution)/shard_map/gather5/pallas_call | solution.py:299
  (40 shorter events, 20.1 us)
Async XLA Ops:
  0.6 14.9 %copy-start = (bf16[256,4608]{1,0:T(8,128)(2,1)S(1)}, bf16[256,4608]{1,0:T(8,128)(2,1)}, u32[]{:S(2)}) copy-start(bf16[256,4608]{1,0:T(8,128)(2,1)} %param.11) | copy-start | bytes 7077892
  5.2 21.5 %all-to-all-start = ((bf16[64,4,2,16]{3,2,1,0:T(2,128)(2,1)}), bf16[64,4,2,16]{3,2,1,0:T(2,128)(2,1)S(1)}, u32[]{:S(2)}, u32[]{:S(2)}) async-start(bf16[64,4,2,16]{3,2,1,0:T(2,128)(2,1)} %bitcast.9), calls=%async_computation | async-start | bytes 262144 | tf_op jit(solution)/shard_map/all_to_all | solution.py:336
  26.6 69.0 %all-to-all-start.2 = ((bf16[64,4,2,4608]{3,2,1,0:T(2,128)(2,1)}), bf16[64,4,2,4608]{3,2,1,0:T(2,128)(2,1)}, u32[]{:S(2)}, u32[]{:S(2)}) async-start(bf16[64,4,2,4608]{3,2,1,0:T(2,128)(2,1)} %reshape.62), calls=%async_computation.2 | async-start | bytes 9437184 | tf_op jit(solution)/shard_map/all_to_all | solution.py:336
  95.6 14.1 %all-to-all-start.1 = ((bf16[4,2,1024]{2,1,0:T(2,128)(2,1)}), bf16[4,2,1024]{2,1,0:T(2,128)(2,1)S(1)}, u32[]{:S(2)}, u32[]{:S(2)}) async-start(bf16[4,2,1024]{2,1,0:T(2,128)(2,1)} %reshape.67), calls=%async_computation.1 | async-start | bytes 32768 | tf_op jit(solution)/shard_map/all_to_all | solution.py:337
  109.7 323.8 %all-to-all-start.3 = ((bf16[64,4,2,4608]{3,0,2,1:T(8,128)(2,1)}), bf16[64,4,2,4608]{3,0,2,1:T(8,128)(2,1)}, u32[]{:S(2)}, u32[]{:S(2)}) async-start(bf16[64,4,2,4608]{3,0,2,1:T(8,128)(2,1)} %copy.21), calls=%async_computation.3 | async-start | bytes 9437184 | tf_op jit(solution)/shard_map/all_to_all | solution.py:337
  115.4 124.8 %copy-start.1 = (s32[14,4096]{1,0:T(8,128)S(1)}, s32[14,4096]{1,0:T(8,128)}, u32[]{:S(2)}) copy-start(s32[14,4096]{1,0:T(8,128)} %refs_0_.5) | copy-start | bytes 688132
  115.4 124.8 %copy-start.2 = (f32[7,4608]{1,0:T(8,128)S(1)}, f32[7,4608]{1,0:T(8,128)}, u32[]{:S(2)}) copy-start(f32[7,4608]{1,0:T(8,128)} %refs_1_.5) | copy-start | bytes 387076
  117.2 123.0 %collective-permute-start = (f32[64,4096]{1,0:T(8,128)S(1)}, f32[64,4096]{1,0:T(8,128)S(1)}, u32[]{:S(2)}, u32[]{:S(2)}) collective-permute-start(f32[64,4096]{1,0:T(8,128)S(1)} %get-tuple-element.20), channel_id=1, source_target_pairs={{0,32},{4,36},{8,40},{12,44},{16,48},{20,52},{24,56},{28,60},{32,0... | collective-permute-start | bytes 3145736 | tf_op jit(solution)/shard_map/ppermute | solution.py:317
  325.9 15.5 %collective-permute-start.1 = (f32[32,4096]{1,0:T(8,128)}, f32[32,4096]{1,0:T(8,128)}, u32[]{:S(2)}, u32[]{:S(2)}) collective-permute-start(f32[32,4096]{1,0:T(8,128)} %get-tuple-element.22), channel_id=1, source_target_pairs={{0,64},{4,68},{8,72},{12,76},{16,80},{20,84},{24,88},{28,92},{32,9... | collective-permute-start | bytes 1572872 | tf_op jit(solution)/shard_map/ppermute | solution.py:317
  431.9 36.9 %copy-start.4 = (s32[512]{0:T(512)S(1)}, s32[512]{0:T(512)}, u32[]{:S(2)}) copy-start(s32[512]{0:T(512)} %param.10) | copy-start | bytes 6148
  432.6 9.6 %collective-permute-start.2 = (f32[16,4096]{1,0:T(8,128)}, f32[16,4096]{1,0:T(8,128)S(1)}, u32[]{:S(2)}, u32[]{:S(2)}) collective-permute-start(f32[16,4096]{1,0:T(8,128)} %get-tuple-element.24), channel_id=1, source_target_pairs={{0,128},{4,132},{8,136},{12,140},{16,144},{20,148},{24,152},{28,15... | collective-permute-start | bytes 786440 | tf_op jit(solution)/shard_map/ppermute | solution.py:317
  483.8 0.7 copy-start.3

commit v2 on v1

--- a/solution.py
+++ b/solution.py
@@ -178,6 +178,7 @@
         out_specs=(VMEM,) * 3,
         scratch_shapes=[pltpu.VMEM((8, U), i32), pltpu.VMEM((8, U + K), f32)],
         compiler_params=pltpu.CompilerParams(vmem_limit_bytes=40 * 2**20),
+        cost_estimate=pl.CostEstimate(flops=2 * 10**9, bytes_accessed=4 * 10**6, transcendentals=0),
         name="assemble%d" % level,
     )(*ins)
 
@@ -232,6 +233,7 @@
         out_specs=VMEM,
         scratch_shapes=[pltpu.VMEM((K, K + 128), f32)],
         compiler_params=pltpu.CompilerParams(vmem_limit_bytes=32 * 2**20),
+        cost_estimate=pl.CostEstimate(flops=10**10, bytes_accessed=40 * 10**6, transcendentals=0),
         name="factor%d" % level,
     )(*ins)
 
@@ -308,6 +310,7 @@
         compiler_params=pltpu.CompilerParams(
             collective_id=ident, has_side_effects=True, vmem_limit_bytes=32 * 2**20
         ),
+        cost_estimate=pl.CostEstimate(flops=10**10, bytes_accessed=60 * 10**6, transcendentals=0),
         name="gather%d" % ident,
     )(piece)
     return out.reshape(-1, cols)
@@ -317,40 +320,59 @@
     return lax.ppermute(shard, "cube", [(i, i ^ 1 << stride) for i in range(64)])
 
 
-def route_rows(coupling_rows, coupling_owner, coupling_slot):
-    cubes, panels, root_rows = 64, PANELS, 16
-    owners = coupling_owner[:, 0]
-    owner_count = cubes * panels
-    owner_hits = (owners[:, None] == jnp.arange(owner_count, dtype=i32)[None, :]).astype(i32)
-    earlier = jnp.sum((jnp.cumsum(owner_hits, axis=0) - owner_hits) * owner_hits, axis=1)
-    target = owners * CAP + earlier
-    row_width = coupling_rows.shape[1]
-    choose = (target[None, :] == jnp.arange(owner_count * CAP, dtype=i32)[:, None]).astype(bf16)
-    marks = (coupling_slot[:, None] == jnp.arange(root_rows, dtype=i32)[None, :]).astype(bf16)
-    outgoing = jnp.dot(choose, coupling_rows, preferred_element_type=f32).astype(bf16)
-    labels = jnp.dot(choose, marks, preferred_element_type=f32).astype(bf16)
-    outgoing = outgoing.reshape(cubes, panels, CAP, row_width)
-    labels = labels.reshape(cubes, panels, CAP, root_rows)
-
-    def spread(v):
-        v = lax.all_to_all(v, "cube", split_axis=0, concat_axis=0, tiled=True)
-        return lax.all_to_all(v, "panel", split_axis=1, concat_axis=1, tiled=True)
-
-    return jnp.einsum("abcr,abcf->rf", spread(labels), spread(outgoing), preferred_element_type=f32)
+def plane_of(owner):
+    cube, zh = owner // PANELS, lax.rem(owner, PANELS)
+    cls = cube // 16 * 8 + lax.rem(cube, 8)
+    return cls, lax.rem(cube // 8, 2) * PANELS + zh
+
+
+def route_plane(coupling_rows, coupling_owner, coupling_slot):
+    cls, z = plane_of(coupling_owner[:, 0])
+    m = coupling_rows.shape[0]
+    hits = (cls[:, None] == jnp.arange(32, dtype=i32)[None, :]).astype(bf16)
+    before = (jnp.arange(m)[:, None] > jnp.arange(m)[None, :]).astype(bf16)
+    earlier = jnp.dot(before, hits, preferred_element_type=f32)
+    earlier = jnp.sum(earlier * hits.astype(f32), axis=1).astype(i32)
+    target = cls * 16 + earlier
+    choose = (target[None, :] == jnp.arange(512, dtype=i32)[:, None]).astype(bf16)
+    marks = (z * 16 + coupling_slot)[:, None] == jnp.arange(128, dtype=i32)[None, :]
+    payload = jnp.concatenate([coupling_rows, marks.astype(bf16)], axis=1)
+    outgoing = jnp.dot(choose, payload, preferred_element_type=f32).astype(bf16)
+    outgoing = outgoing.reshape(32, 16, -1)
+    groups = [[y * 16 + zl * 8 + xc for y in range(4) for xc in range(8)] for zl in range(2)]
+    return lax.all_to_all(outgoing, "cube", 0, 0, axis_index_groups=groups, tiled=True)
+
+
+def route_column(got):
+    got = got.reshape(512, -1)
+    sums = lax.dot_general(
+        got[:, U + K:], got[:, :U + K], (((0,), (0,)), ((), ())), preferred_element_type=f32
+    ).astype(bf16).reshape(8, 16, U + K)
+    groups = [
+        [(y * 16 + zl * 8 + xc) * PANELS + zh for zl in range(2) for zh in range(PANELS)]
+        for y in range(4) for xc in range(8)
+    ]
+    return lax.all_to_all(sums, ("cube", "panel"), 0, 0, axis_index_groups=groups, tiled=True)
 
 
 def body(leaf_updates, extend_maps, front_diagonal, pivot_order, coupling_rows, coupling_owner, coupling_slot):
-    assembly = route_rows(coupling_rows, coupling_owner, coupling_slot)
+    routed = route_plane(coupling_rows, coupling_owner, coupling_slot)
+    assembly = None
     children = leaf_updates
     order = pivot_order.reshape(1, K)
     for level in range(3):
         r = children.shape[0] // 2
         incoming = from_partner(children[r:], 3 + level)
+        if level == 2:
+            assembly = jnp.sum(routed.astype(f32), axis=0)
         piece, coupled, update_rows = assemble(
             level, extend_maps, front_diagonal, children[:r], incoming, assembly
         )
         pivots = gather(level, piece, 2 * level)
         factor = make_factor(level, pivots, coupled, order)
+        if level == 0:
+            routed, factor = lax.optimization_barrier((routed, factor))
+            routed = route_column(routed)
         collected = gather(level, factor, 2 * level + 1)
         product = lax.dot_general(
             factor, collected, (((1,), (1,)), ((), ())), preferred_element_type=f32

time: 539 us -> 371 us (0.69)
  waiting for transfers between devices: 200 us -> 35.6 us
  Pallas kernels: 259 us -> 295 us
  starting transfers between devices: 37.1 us -> 17 us
  local copies, waits for them, and re-layouts: 20.1 us -> 0.99 us
    ppermute x3, waiting for transfers between devices: 140 us -> 35.6 us  [from_partner(): lax.ppermute(shard, 'cube', [(i, i ^ 1 << stride) for i in range(64)])]
    all_to_all x4 -> x2, waiting for transfers between devices: 60.1 us -> 0.01 us  [the longest x1 0.01 us: route_plane(): lax.all_to_all(outgoing, 'cube', 0, 0, axis_index_groups=groups, tiled=True)]
    pallas_call x6, Pallas kernels: 205 us -> 242 us  [gather(): pl.pallas_call(functools.partial(gather_kernel, ysize), out_shape=jax.Sha...]
    all_to_all x4 -> x2, starting transfers between devices: 32.3 us -> 12.3 us  [the longest x1 8.77 us: route_plane(): lax.all_to_all(outgoing, 'cube', 0, 0, axis_index_groups=groups, tiled=True)]
    reshape x1 -> x0, local copies, waits for them, and re-layouts: 7.52 us -> none  [route_rows(): outgoing = outgoing.reshape(cubes, panels, CAP, row_width)]
    all_to_all x2 -> x0, local copies, waits for them, and re-layouts: 5.95 us -> none  [spread(): v = lax.all_to_all(v, 'cube', split_axis=0, concat_axis=0, tiled=True)]
  transfers between devices with their start and end apart: 7 -> 5, of which waited for: 5 -> 3; matrix products, arithmetic and copies ran while one was open for 5% -> 2% of each run, Pallas kernels for 32% -> 44%
where the time goes in v2:
time: 371 us; the launch traced here: 366 us
  Pallas kernels  295 us (80%)
  waiting for transfers between devices  35.6 us (10%)
  starting transfers between devices  17 us (5%)
  matrix products  13.7 us (4%)
    pallas_call x6, Pallas kernels, gather(): pl.pallas_call(functools.partial(gather_kernel, ysize), out_shape=jax.Sha...  242 us
    pallas_call x3, Pallas kernels, make_factor(): pl.pallas_call(functools.partial(factor_kernel, level), out_shape=jax.Sha...  40.8 us
    ppermute x3, waiting for transfers between devices, from_partner(): lax.ppermute(shard, 'cube', [(i, i ^ 1 << stride) for i in range(64)])  35.6 us
    pallas_call x3, Pallas kernels, assemble(): pl.pallas_call(functools.partial(assemble_kernel, level), out_shape=(jax....  12.2 us
    all_to_all x1, starting transfers between devices, route_plane(): lax.all_to_all(outgoing, 'cube', 0, 0, axis_index_groups=groups, tiled=True)  8.77 us
  transfers between devices with their start and end apart: 5, of which 3 were waited for; matrix products, arithmetic and copies ran while one was open for 2% of the time, Pallas kernels for 44%

profile of v2, /device:TPU:1, one launch (start us, length us, event | category | flops | bytes accessed | tf_op | source)
XLA Modules:
  0.0 366.4 jit_solution(10126201753076381307)
XLA Ops:
  2.4 5.4 %convolution_convert_fusion = bf16[512,4736]{1,0:T(8,128)(2,1)} fusion(bf16[256,128]{1,0:T(8,128)(2,1)S(1)} %fusion.7, bf16[256,4608]{1,0:T(8,128)(2,1)} %param.11, s32[256]{0:T(256)S(1)} %get-tuple-element.30), kind=kOutput, calls=%fused_computation | convolution fusion | flops 1248919552 | bytes 7275520 | tf_op jit(solution)/shard_map/dot_general | solution.py:340
  7.7 8.8 %all-to-all-start = ((bf16[32,16,4736]{2,1,0:T(8,128)(2,1)}), bf16[32,16,4736]{2,1,0:T(8,128)(2,1)}, u32[]{:S(2)}, u32[]{:S(2)}) async-start(bf16[32,16,4736]{2,1,0:T(8,128)(2,1)} %bitcast.25), calls=%async_computation | async-start | bytes 9699328 | tf_op jit(solution)/shard_map/all_to_all | solution.py:343
  16.7 1.7 collective-permute-start
  18.4 23.3 %collective-permute-done.refs_3_ = f32[64,4096]{1,0:T(8,128)S(1)} collective-permute-done((f32[64,4096]{1,0:T(8,128)S(1)}, f32[64,4096]{1,0:T(8,128)S(1)}, u32[]{:S(2)}, u32[]{:S(2)}) %collective-permute-start) | collective-permute-done | bytes 1048608 | tf_op jit(solution)/shard_map/ppermute | solution.py:320
  41.7 4.4 %assemble0.1 = (f32[32,128]{1,0:T(8,128)S(1)}, f32[64,512]{1,0:T(8,128)S(1)}, f32[64,4096]{1,0:T(8,128)S(1)}) custom-call(s32[14,4096]{1,0:T(8,128)S(1)} %copy-done.1, f32[7,4608]{1,0:T(8,128)S(1)} %copy-done.2, f32[64,4096]{1,0:T(8,128)S(1)} %get-tuple-element.25.refs_2_, f32[64,4096]{1,0:T(8,128)S(1)} %collective-permute-done.refs_3_), custom_call_target="tpu_custom_call" | custom-call | flops 2000000000 | bytes 4000000 | tf_op jit(solution)/shard_map/assemble0/pallas_call | solution.py:170
  46.1 36.6 %gather0.1 = f32[1,2,4,2,4,32,128]{6,5,4,3,2,1,0:T(8,128)S(1)} custom-call(f32[32,128]{1,0:T(8,128)S(1)} %get-tuple-element.14.x_ref), custom_call_target="tpu_custom_call" | custom-call | flops 10000000000 | bytes 60000000 | tf_op jit(solution)/shard_map/gather0/pallas_call | solution.py:301
  82.7 12.9 %factor0.1.x_ref = bf16[64,512]{1,0:T(8,128)(2,1)S(1)} custom-call(f32[2048,128]{1,0:T(8,128)S(1)} %bitcast.22, f32[64,512]{1,0:T(8,128)S(1)} %get-tuple-element.15.refs_1_), custom_call_target="tpu_custom_call" | custom-call | flops 10000000000 | bytes 40000000 | tf_op jit(solution)/shard_map/factor0/pallas_call | solution.py:229
  95.6 50.2 %gather1.1 = bf16[1,2,4,2,4,64,512]{6,5,4,3,2,1,0:T(8,128)(2,1)S(1)} custom-call(bf16[64,512]{1,0:T(8,128)(2,1)S(1)} %factor0.1.x_ref), custom_call_target="tpu_custom_call" | custom-call | flops 10000000000 | bytes 60000000 | tf_op jit(solution)/shard_map/gather1/pallas_call | solution.py:301
  145.8 1.4 fusion.18
  147.5 1.3 collective-permute-start.1
  148.8 4.3 %convolution_convert_fusion.1 = bf16[128,4608]{1,0:T(8,128)(2,1)} fusion(bf16[512,4736]{1,0:T(8,128)(2,1)} %bitcast.7), kind=kOutput, calls=%fused_computation.1 | convolution fusion | flops 604569600 | bytes 6029312 | tf_op jit(solution)/shard_map/dot_general | solution.py:348
  153.1 3.6 all-to-all-start.1
  156.6 4.5 %collective-permute-done.1.refs_3_ = f32[32,4096]{1,0:T(8,128)S(1)} collective-permute-done((f32[32,4096]{1,0:T(8,128)S(1)}, f32[32,4096]{1,0:T(8,128)S(1)}, u32[]{:S(2)}, u32[]{:S(2)}) %collective-permute-start.1) | collective-permute-done | bytes 524320 | tf_op jit(solution)/shard_map/ppermute | solution.py:320
  161.1 4.0 %assemble1.1 = (f32[16,128]{1,0:T(8,128)S(1)}, f32[32,512]{1,0:T(8,128)S(1)}, f32[32,4096]{1,0:T(8,128)S(1)}) custom-call(s32[14,4096]{1,0:T(8,128)S(1)} %copy-done.1, f32[7,4608]{1,0:T(8,128)S(1)} %copy-done.2, f32[32,4096]{1,0:T(8,128)S(1)} %get-tuple-element.27.refs_2_, f32[32,4096]{1,0:T(8,128)S(1)} %collective-permute-done.1.refs_3_), custom_call_target="tpu_custom_call" | custom-call | flops 2000000000 | bytes 4000000 | tf_op jit(solution)/shard_map/assemble1/pallas_call | solution.py:170
  165.1 37.2 %gather2.1 = f32[2,2,4,2,4,16,128]{6,5,4,3,2,1,0:T(8,128)S(1)} custom-call(f32[16,128]{1,0:T(8,128)S(1)} %get-tuple-element.18.x_ref), custom_call_target="tpu_custom_call" | custom-call | flops 10000000000 | bytes 60000000 | tf_op jit(solution)/shard_map/gather2/pallas_call | solution.py:301
  202.3 12.9 %factor1.1.x_ref = bf16[32,512]{1,0:T(8,128)(2,1)S(1)} custom-call(f32[2048,128]{1,0:T(8,128)S(1)} %bitcast.23, f32[32,512]{1,0:T(8,128)S(1)} %get-tuple-element.19.refs_1_), custom_call_target="tpu_custom_call" | custom-call | flops 10000000000 | bytes 40000000 | tf_op jit(solution)/shard_map/factor1/pallas_call | solution.py:229
  215.2 53.1 %gather3.1 = bf16[2,2,4,2,4,32,512]{6,5,4,3,2,1,0:T(8,128)(2,1)S(1)} custom-call(bf16[32,512]{1,0:T(8,128)(2,1)S(1)} %factor1.1.x_ref), custom_call_target="tpu_custom_call" | custom-call | flops 10000000000 | bytes 60000000 | tf_op jit(solution)/shard_map/gather3/pallas_call | solution.py:301
  268.4 1.3 fusion.19
  269.8 1.6 collective-permute-start.2
  271.6 7.8 %collective-permute-done.2.refs_3_ = f32[16,4096]{1,0:T(8,128)S(1)} collective-permute-done((f32[16,4096]{1,0:T(8,128)S(1)}, f32[16,4096]{1,0:T(8,128)S(1)}, u32[]{:S(2)}, u32[]{:S(2)}) %collective-permute-start.2) | collective-permute-done | bytes 262176 | tf_op jit(solution)/shard_map/ppermute | solution.py:320
  279.4 3.8 %assemble2.1 = (f32[8,128]{1,0:T(8,128)S(1)}, f32[16,512]{1,0:T(8,128)S(1)}, f32[16,4096]{1,0:T(8,128)S(1)}) custom-call(s32[14,4096]{1,0:T(8,128)S(1)} %copy-done.1, f32[7,4608]{1,0:T(8,128)S(1)} %copy-done.2, f32[16,4096]{1,0:T(8,128)S(1)} %get-tuple-element.29.refs_2_, f32[16,4096]{1,0:T(8,128)S(1)} %collective-permute-done.2.refs_3_, ...), custom_call_target="tpu_custom_call" | custom-call | flops 2000000000 | bytes 4000000 | tf_op jit(solution)/shard_map/assemble2/pallas_call | solution.py:170
  283.2 22.4 %gather4.1 = f32[4,2,4,2,4,8,128]{6,5,4,3,2,1,0:T(8,128)S(1)} custom-call(f32[8,128]{1,0:T(8,128)S(1)} %get-tuple-element.21.x_ref), custom_call_target="tpu_custom_call" | custom-call | flops 10000000000 | bytes 60000000 | tf_op jit(solution)/shard_map/gather4/pallas_call | solution.py:301
  305.6 15.0 %factor2.1.x_ref = bf16[16,512]{1,0:T(8,128)(2,1)} custom-call(f32[2048,128]{1,0:T(8,128)S(1)} %bitcast.24, f32[16,512]{1,0:T(8,128)S(1)} %get-tuple-element.22.refs_1_, s32[1,512]{1,0:T(1,128)S(1)} %bitcast.21), custom_call_target="tpu_custom_call" | custom-call | flops 10000000000 | bytes 40000000 | tf_op jit(solution)/shard_map/factor2/pallas_call | solution.py:229
  321.3 42.9 %gather5.1 = bf16[4,2,4,2,4,16,512]{6,5,4,3,2,1,0:T(8,128)(2,1)S(1)} custom-call(bf16[16,512]{1,0:T(8,128)(2,1)S(1)} %copy-done), custom_call_target="tpu_custom_call" | custom-call | flops 10000000000 | bytes 60000000 | tf_op jit(solution)/shard_map/gather5/pallas_call | solution.py:301
  (24 shorter events, 5.0 us)
Async XLA Ops:
  7.7 8.8 %copy-start.4 = (f32[128,4096]{1,0:T(8,128)S(1)}, f32[128,4096]{1,0:T(8,128)}, u32[]{:S(2)}) copy-start(f32[128,4096]{1,0:T(8,128)} %param.7) | copy-start | bytes 6291460
  7.7 87.9 %all-to-all-start = ((bf16[32,16,4736]{2,1,0:T(8,128)(2,1)}), bf16[32,16,4736]{2,1,0:T(8,128)(2,1)}, u32[]{:S(2)}, u32[]{:S(2)}) async-start(bf16[32,16,4736]{2,1,0:T(8,128)(2,1)} %bitcast.25), calls=%async_computation | async-start | bytes 9699328 | tf_op jit(solution)/shard_map/all_to_all | solution.py:343
  16.5 25.2 %copy-start.1 = (s32[14,4096]{1,0:T(8,128)S(1)}, s32[14,4096]{1,0:T(8,128)}, u32[]{:S(2)}) copy-start(s32[14,4096]{1,0:T(8,128)} %refs_0_.5) | copy-start | bytes 688132
  16.5 25.2 %copy-start.2 = (f32[7,4608]{1,0:T(8,128)S(1)}, f32[7,4608]{1,0:T(8,128)}, u32[]{:S(2)}) copy-start(f32[7,4608]{1,0:T(8,128)} %refs_1_.5) | copy-start | bytes 387076
  16.7 25.0 %collective-permute-start = (f32[64,4096]{1,0:T(8,128)S(1)}, f32[64,4096]{1,0:T(8,128)S(1)}, u32[]{:S(2)}, u32[]{:S(2)}) collective-permute-start(f32[64,4096]{1,0:T(8,128)S(1)} %get-tuple-element.24), channel_id=1, source_target_pairs={{0,32},{4,36},{8,40},{12,44},{16,48},{20,52},{24,56},{28,60},{32,0... | collective-permute-start | bytes 3145736 | tf_op jit(solution)/shard_map/ppermute | solution.py:320
  147.5 13.6 %collective-permute-start.1 = (f32[32,4096]{1,0:T(8,128)S(1)}, f32[32,4096]{1,0:T(8,128)S(1)}, u32[]{:S(2)}, u32[]{:S(2)}) collective-permute-start(f32[32,4096]{1,0:T(8,128)S(1)} %get-tuple-element.26), channel_id=1, source_target_pairs={{0,64},{4,68},{8,72},{12,76},{16,80},{20,84},{24,88},{28,92},{32,9... | collective-permute-start | bytes 1572872 | tf_op jit(solution)/shard_map/ppermute | solution.py:320
  153.1 118.3 %all-to-all-start.1 = ((bf16[8,16,4608]{2,1,0:T(8,128)(2,1)}), bf16[8,16,4608]{2,1,0:T(8,128)(2,1)S(1)}, u32[]{:S(2)}, u32[]{:S(2)}) async-start(bf16[8,16,4608]{2,1,0:T(8,128)(2,1)} %bitcast.26), calls=%async_computation.1 | async-start | bytes 2359296 | tf_op jit(solution)/shard_map/all_to_all | solution.py:355
  269.8 9.6 %collective-permute-start.2 = (f32[16,4096]{1,0:T(8,128)S(1)}, f32[16,4096]{1,0:T(8,128)S(1)}, u32[]{:S(2)}, u32[]{:S(2)}) collective-permute-start(f32[16,4096]{1,0:T(8,128)S(1)} %get-tuple-element.28), channel_id=1, source_target_pairs={{0,128},{4,132},{8,136},{12,140},{16,144},{20,148},{24,152},{28,15... | collective-permute-start | bytes 786440 | tf_op jit(solution)/shard_map/ppermute | solution.py:320
  283.2 22.4 %copy-start.3 = (s32[512]{0:T(512)S(1)}, s32[512]{0:T(512)}, u32[]{:S(2)}) copy-start(s32[512]{0:T(512)} %param.10) | copy-start | bytes 6148
  320.6 0.7 copy-start

commit v3 on v2

--- a/solution.py
+++ b/solution.py
@@ -316,6 +316,89 @@
     return out.reshape(-1, cols)
 
 
+def update_kernel(ysize, f_ref, upd_ref, out, fi, fj, prod, got, send_sem, recv_sem):
+    r = f_ref.shape[0]
+    cube_at = lax.axis_index("cube")
+    zh = lax.axis_index("panel")
+    w = lax.rem(cube_at, 8)
+    zl = lax.rem(cube_at // 8, 2)
+    yfull = cube_at // 16
+    y = lax.rem(yfull, ysize)
+    ybase = yfull - y
+
+    def target(y, zl, w, zh):
+        return {"cube": (ybase + y) * 16 + zl * 8 + w, "panel": zh}
+
+    mine = (y * 2 + zl) * PANELS + zh
+    v_peers = [
+        target(lax.rem(y + a, ysize), lax.rem(zl + b, 2), w, lax.rem(zh + c, 4))
+        for a in range(ysize) for b in range(2) for c in range(4) if a + b + c
+    ]
+    w_places = [lax.rem(w + d, 8) for d in range(1, 8)]
+    w_peers = [target(y, zl, place, zh) for place in w_places]
+    barrier = pltpu.get_barrier_semaphore()
+    for peer in v_peers + w_peers:
+        pl.semaphore_signal(barrier, inc=1, device_id=peer, device_id_type=pl.DeviceIdType.MESH)
+    fi[pl.ds(w, 1)] = f_ref[...][None]
+    fj[pl.ds(mine, 1)] = f_ref[...][None]
+    pl.semaphore_wait(barrier, len(v_peers) + len(w_peers))
+    copies = []
+
+    def send(src, dst, peer):
+        copy = pltpu.make_async_remote_copy(
+            src_ref=src, dst_ref=dst, send_sem=send_sem.at[len(copies)], recv_sem=recv_sem.at[len(copies)],
+            device_id=peer, device_id_type=pl.DeviceIdType.MESH,
+        )
+        copy.start()
+        copies.append(copy)
+
+    for peer in v_peers:
+        send(fj.at[mine], fj.at[mine], peer)
+    for peer in w_peers:
+        send(fi.at[w], fi.at[w], peer)
+    for copy in copies:
+        copy.wait_recv()
+    right = fj[...].reshape(-1, K)
+    prod[...] = lax.dot_general(
+        fi[...].reshape(-1, K), right, (((1,), (1,)), ((), ())), preferred_element_type=f32
+    ).reshape(8, r, 512)
+    first = len(copies)
+    for place, peer in zip(w_places, w_peers):
+        send(prod.at[place], got.at[w], peer)
+    got[pl.ds(w, 1)] = prod[pl.ds(w, 1)]
+    for copy in copies[first:]:
+        copy.wait_recv()
+    wide = PANELS * r
+    for block in range(2 * ysize):
+        parts = [got[q, :, block * wide:(block + 1) * wide] for q in range(8)]
+        lo = block * 8 * wide
+        out[:, lo:lo + 8 * wide] = upd_ref[:, lo:lo + 8 * wide] - jnp.concatenate(parts, axis=1)
+    for copy in copies:
+        copy.wait_send()
+
+
+def update(level, factor, update_rows, ident):
+    ysize = 1 << level
+    r = factor.shape[0]
+    count = 8 * ysize - 1 + 7 + 7
+    return pl.pallas_call(
+        functools.partial(update_kernel, ysize),
+        out_shape=jax.ShapeDtypeStruct((r, U), f32),
+        in_specs=[VMEM] * 2,
+        out_specs=VMEM,
+        scratch_shapes=[
+            pltpu.VMEM((8, r, K), bf16), pltpu.VMEM((8 * ysize, r, K), bf16),
+            pltpu.VMEM((8, r, 512), f32), pltpu.VMEM((8, r, 512), f32),
+            pltpu.SemaphoreType.DMA((count,)), pltpu.SemaphoreType.DMA((count,)),
+        ],
+        compiler_params=pltpu.CompilerParams(
+            collective_id=ident, has_side_effects=True, vmem_limit_bytes=32 * 2**20
+        ),
+        cost_estimate=pl.CostEstimate(flops=10**10, bytes_accessed=60 * 10**6, transcendentals=0),
+        name="update%d" % level,
+    )(factor, update_rows)
+
+
 def from_partner(shard, stride):
     return lax.ppermute(shard, "cube", [(i, i ^ 1 << stride) for i in range(64)])
 
@@ -373,11 +456,7 @@
         if level == 0:
             routed, factor = lax.optimization_barrier((routed, factor))
             routed = route_column(routed)
-        collected = gather(level, factor, 2 * level + 1)
-        product = lax.dot_general(
-            factor, collected, (((1,), (1,)), ((), ())), preferred_element_type=f32
-        )
-        children = update_rows - product
+        children = update(level, factor, update_rows, 2 * level + 1)
     return (factor, children)
 
 

time: 371 us -> 308 us (0.83)
  Pallas kernels: 295 us -> 237 us
  matrix products: 13.7 us -> 9.84 us
    pallas_call x6 -> x3, Pallas kernels: 242 us -> 100 us  [gather(): pl.pallas_call(functools.partial(gather_kernel, ysize), out_shape=jax.Sha...]
    pallas_call x0 -> x3, Pallas kernels: none -> 83.4 us  [update(): pl.pallas_call(functools.partial(update_kernel, ysize), out_shape=jax.Sha...]
    dot_general x3 -> x0, matrix products: 3.87 us -> none  [body(): lax.dot_general(factor, collected, (((1,), (1,)), ((), ())), preferred_el...]
where the time goes in v3:
time: 308 us; the launch traced here: 303 us
  Pallas kernels  237 us (77%)
  waiting for transfers between devices  33.8 us (11%)
  starting transfers between devices  18.4 us (6%)
  matrix products  9.84 us (3%)
    pallas_call x3, Pallas kernels, gather(): pl.pallas_call(functools.partial(gather_kernel, ysize), out_shape=jax.Sha...  100 us
    pallas_call x3, Pallas kernels, update(): pl.pallas_call(functools.partial(update_kernel, ysize), out_shape=jax.Sha...  83.4 us
    pallas_call x3, Pallas kernels, make_factor(): pl.pallas_call(functools.partial(factor_kernel, level), out_shape=jax.Sha...  40.8 us
    ppermute x3, waiting for transfers between devices, from_partner(): lax.ppermute(shard, 'cube', [(i, i ^ 1 << stride) for i in range(64)])  33.8 us
    pallas_call x3, Pallas kernels, assemble(): pl.pallas_call(functools.partial(assemble_kernel, level), out_shape=(jax....  12.2 us
    all_to_all x1, starting transfers between devices, route_plane(): lax.all_to_all(outgoing, 'cube', 0, 0, axis_index_groups=groups, tiled=True)  8.77 us
  transfers between devices with their start and end apart: 5, of which 3 were waited for; matrix products, arithmetic and copies ran while one was open for 2% of the time, Pallas kernels for 44%

profile of v3, /device:TPU:1, one launch (start us, length us, event | category | flops | bytes accessed | tf_op | source)
XLA Modules:
  0.0 303.1 jit_solution(7146003570064527347)
XLA Ops:
  1.5 0.7 convert_add_fusion
  2.4 5.4 %convolution_convert_fusion = bf16[512,4736]{1,0:T(8,128)(2,1)} fusion(bf16[256,128]{1,0:T(8,128)(2,1)S(1)} %fusion.7, bf16[256,4608]{1,0:T(8,128)(2,1)} %param.11, s32[256]{0:T(256)S(1)} %get-tuple-element.30), kind=kOutput, calls=%fused_computation | convolution fusion | flops 1248919552 | bytes 7275520 | tf_op jit(solution)/shard_map/dot_general | solution.py:423
  7.7 8.8 %all-to-all-start = ((bf16[32,16,4736]{2,1,0:T(8,128)(2,1)}), bf16[32,16,4736]{2,1,0:T(8,128)(2,1)}, u32[]{:S(2)}, u32[]{:S(2)}) async-start(bf16[32,16,4736]{2,1,0:T(8,128)(2,1)} %bitcast.13), calls=%async_computation | async-start | bytes 9699328 | tf_op jit(solution)/shard_map/all_to_all | solution.py:426
  16.7 1.7 collective-permute-start
  18.5 23.3 %collective-permute-done.refs_3_ = f32[64,4096]{1,0:T(8,128)S(1)} collective-permute-done((f32[64,4096]{1,0:T(8,128)S(1)}, f32[64,4096]{1,0:T(8,128)S(1)}, u32[]{:S(2)}, u32[]{:S(2)}) %collective-permute-start) | collective-permute-done | bytes 1048608 | tf_op jit(solution)/shard_map/ppermute | solution.py:403
  41.8 4.4 %assemble0.1 = (f32[32,128]{1,0:T(8,128)S(1)}, f32[64,512]{1,0:T(8,128)S(1)}, f32[64,4096]{1,0:T(8,128)S(1)}) custom-call(s32[14,4096]{1,0:T(8,128)S(1)} %copy-done, f32[7,4608]{1,0:T(8,128)S(1)} %copy-done.1, f32[64,4096]{1,0:T(8,128)S(1)} %get-tuple-element.25.refs_2_, f32[64,4096]{1,0:T(8,128)S(1)} %collective-permute-done.refs_3_), custom_call_target="tpu_custom_call" | custom-call | flops 2000000000 | bytes 4000000 | tf_op jit(solution)/shard_map/assemble0/pallas_call | solution.py:170
  46.2 36.5 %gather0.1 = f32[1,2,4,2,4,32,128]{6,5,4,3,2,1,0:T(8,128)S(1)} custom-call(f32[32,128]{1,0:T(8,128)S(1)} %get-tuple-element.13.x_ref), custom_call_target="tpu_custom_call" | custom-call | flops 10000000000 | bytes 60000000 | tf_op jit(solution)/shard_map/gather0/pallas_call | solution.py:301
  82.7 12.9 %factor0.1.f_ref = bf16[64,512]{1,0:T(8,128)(2,1)S(1)} custom-call(f32[2048,128]{1,0:T(8,128)S(1)} %bitcast.10, f32[64,512]{1,0:T(8,128)S(1)} %get-tuple-element.14.refs_1_), custom_call_target="tpu_custom_call" | custom-call | flops 10000000000 | bytes 40000000 | tf_op jit(solution)/shard_map/factor0/pallas_call | solution.py:229
  95.6 35.5 %update0.1 = f32[64,4096]{1,0:T(8,128)S(1)} custom-call(bf16[64,512]{1,0:T(8,128)(2,1)S(1)} %factor0.1.f_ref, f32[64,4096]{1,0:T(8,128)S(1)} %get-tuple-element.16.upd_ref), custom_call_target="tpu_custom_call" | custom-call | flops 10000000000 | bytes 60000000 | tf_op jit(solution)/shard_map/update0/pallas_call | solution.py:384
  131.2 1.1 collective-permute-start.1
  132.3 4.3 %convolution_convert_fusion.1 = bf16[128,4608]{1,0:T(8,128)(2,1)} fusion(bf16[512,4736]{1,0:T(8,128)(2,1)} %bitcast.5), kind=kOutput, calls=%fused_computation.1 | convolution fusion | flops 604569600 | bytes 6029312 | tf_op jit(solution)/shard_map/dot_general | solution.py:431
  136.6 3.6 %all-to-all-start.1 = ((bf16[8,16,4608]{2,1,0:T(8,128)(2,1)}), bf16[8,16,4608]{2,1,0:T(8,128)(2,1)S(1)}, u32[]{:S(2)}, u32[]{:S(2)}) async-start(bf16[8,16,4608]{2,1,0:T(8,128)(2,1)} %bitcast.14), calls=%async_computation.1 | async-start | bytes 2359296 | tf_op jit(solution)/shard_map/all_to_all | solution.py:438
  140.1 4.1 %collective-permute-done.1.refs_3_ = f32[32,4096]{1,0:T(8,128)S(1)} collective-permute-done((f32[32,4096]{1,0:T(8,128)S(1)}, f32[32,4096]{1,0:T(8,128)S(1)}, u32[]{:S(2)}, u32[]{:S(2)}) %collective-permute-start.1) | collective-permute-done | bytes 524320 | tf_op jit(solution)/shard_map/ppermute | solution.py:403
  144.2 4.0 %assemble1.1 = (f32[16,128]{1,0:T(8,128)S(1)}, f32[32,512]{1,0:T(8,128)S(1)}, f32[32,4096]{1,0:T(8,128)S(1)}) custom-call(s32[14,4096]{1,0:T(8,128)S(1)} %copy-done, f32[7,4608]{1,0:T(8,128)S(1)} %copy-done.1, f32[32,4096]{1,0:T(8,128)S(1)} %get-tuple-element.27.refs_2_, f32[32,4096]{1,0:T(8,128)S(1)} %collective-permute-done.1.refs_3_), custom_call_target="tpu_custom_call" | custom-call | flops 2000000000 | bytes 4000000 | tf_op jit(solution)/shard_map/assemble1/pallas_call | solution.py:170
  148.3 39.8 %gather2.1 = f32[2,2,4,2,4,16,128]{6,5,4,3,2,1,0:T(8,128)S(1)} custom-call(f32[16,128]{1,0:T(8,128)S(1)} %get-tuple-element.17.x_ref), custom_call_target="tpu_custom_call" | custom-call | flops 10000000000 | bytes 60000000 | tf_op jit(solution)/shard_map/gather2/pallas_call | solution.py:301
  188.1 12.9 %factor1.1.f_ref = bf16[32,512]{1,0:T(8,128)(2,1)S(1)} custom-call(f32[2048,128]{1,0:T(8,128)S(1)} %bitcast.11, f32[32,512]{1,0:T(8,128)S(1)} %get-tuple-element.18.refs_1_), custom_call_target="tpu_custom_call" | custom-call | flops 10000000000 | bytes 40000000 | tf_op jit(solution)/shard_map/factor1/pallas_call | solution.py:229
  201.0 23.9 %update1.1 = f32[32,4096]{1,0:T(8,128)S(1)} custom-call(bf16[32,512]{1,0:T(8,128)(2,1)S(1)} %factor1.1.f_ref, f32[32,4096]{1,0:T(8,128)S(1)} %get-tuple-element.19.upd_ref), custom_call_target="tpu_custom_call" | custom-call | flops 10000000000 | bytes 60000000 | tf_op jit(solution)/shard_map/update1/pallas_call | solution.py:384
  224.9 3.2 %collective-permute-start.2 = (f32[16,4096]{1,0:T(8,128)S(1)}, f32[16,4096]{1,0:T(8,128)S(1)}, u32[]{:S(2)}, u32[]{:S(2)}) collective-permute-start(f32[16,4096]{1,0:T(8,128)S(1)} %get-tuple-element.28), channel_id=1, source_target_pairs={{0,128},{4,132},{8,136},{12,140},{16,144},{20,148},{24,152},{28,15... | collective-permute-start | bytes 786440 | tf_op jit(solution)/shard_map/ppermute | solution.py:403
  228.2 6.4 %collective-permute-done.2.refs_3_ = f32[16,4096]{1,0:T(8,128)S(1)} collective-permute-done((f32[16,4096]{1,0:T(8,128)S(1)}, f32[16,4096]{1,0:T(8,128)S(1)}, u32[]{:S(2)}, u32[]{:S(2)}) %collective-permute-start.2) | collective-permute-done | bytes 262176 | tf_op jit(solution)/shard_map/ppermute | solution.py:403
  234.6 3.8 %assemble2.1 = (f32[8,128]{1,0:T(8,128)S(1)}, f32[16,512]{1,0:T(8,128)S(1)}, f32[16,4096]{1,0:T(8,128)S(1)}) custom-call(s32[14,4096]{1,0:T(8,128)S(1)} %copy-done, f32[7,4608]{1,0:T(8,128)S(1)} %copy-done.1, f32[16,4096]{1,0:T(8,128)S(1)} %get-tuple-element.29.refs_2_, f32[16,4096]{1,0:T(8,128)S(1)} %collective-permute-done.2.refs_3_, ...), custom_call_target="tpu_custom_call" | custom-call | flops 2000000000 | bytes 4000000 | tf_op jit(solution)/shard_map/assemble2/pallas_call | solution.py:170
  238.4 23.9 %gather4.1 = f32[4,2,4,2,4,8,128]{6,5,4,3,2,1,0:T(8,128)S(1)} custom-call(f32[8,128]{1,0:T(8,128)S(1)} %get-tuple-element.21.x_ref), custom_call_target="tpu_custom_call" | custom-call | flops 10000000000 | bytes 60000000 | tf_op jit(solution)/shard_map/gather4/pallas_call | solution.py:301
  262.3 15.0 %factor2.1.f_ref = bf16[16,512]{1,0:T(8,128)(2,1)} custom-call(f32[2048,128]{1,0:T(8,128)S(1)} %bitcast.12, f32[16,512]{1,0:T(8,128)S(1)} %get-tuple-element.22.refs_1_, s32[1,512]{1,0:T(1,128)S(1)} %bitcast.9), custom_call_target="tpu_custom_call" | custom-call | flops 10000000000 | bytes 40000000 | tf_op jit(solution)/shard_map/factor2/pallas_call | solution.py:229
  277.4 0.7 copy-done.3
  278.1 24.1 %update2.1 = f32[16,4096]{1,0:T(8,128)S(1)} custom-call(bf16[16,512]{1,0:T(8,128)(2,1)S(1)} %copy-done.3, f32[16,4096]{1,0:T(8,128)S(1)} %get-tuple-element.23.upd_ref), custom_call_target="tpu_custom_call" | custom-call | flops 10000000000 | bytes 60000000 | tf_op jit(solution)/shard_map/update2/pallas_call | solution.py:384
  (19 shorter events, 2.2 us)
Async XLA Ops:
  7.7 8.8 %copy-start.4 = (f32[128,4096]{1,0:T(8,128)S(1)}, f32[128,4096]{1,0:T(8,128)}, u32[]{:S(2)}) copy-start(f32[128,4096]{1,0:T(8,128)} %param.7) | copy-start | bytes 6291460
  7.7 87.9 %all-to-all-start = ((bf16[32,16,4736]{2,1,0:T(8,128)(2,1)}), bf16[32,16,4736]{2,1,0:T(8,128)(2,1)}, u32[]{:S(2)}, u32[]{:S(2)}) async-start(bf16[32,16,4736]{2,1,0:T(8,128)(2,1)} %bitcast.13), calls=%async_computation | async-start | bytes 9699328 | tf_op jit(solution)/shard_map/all_to_all | solution.py:426
  16.5 25.2 %copy-start = (s32[14,4096]{1,0:T(8,128)S(1)}, s32[14,4096]{1,0:T(8,128)}, u32[]{:S(2)}) copy-start(s32[14,4096]{1,0:T(8,128)} %refs_0_.5) | copy-start | bytes 688132
  16.5 25.2 %copy-start.1 = (f32[7,4608]{1,0:T(8,128)S(1)}, f32[7,4608]{1,0:T(8,128)}, u32[]{:S(2)}) copy-start(f32[7,4608]{1,0:T(8,128)} %refs_1_.5) | copy-start | bytes 387076
  16.7 25.0 %collective-permute-start = (f32[64,4096]{1,0:T(8,128)S(1)}, f32[64,4096]{1,0:T(8,128)S(1)}, u32[]{:S(2)}, u32[]{:S(2)}) collective-permute-start(f32[64,4096]{1,0:T(8,128)S(1)} %get-tuple-element.24), channel_id=1, source_target_pairs={{0,32},{4,36},{8,40},{12,44},{16,48},{20,52},{24,56},{28,60},{32,0... | collective-permute-start | bytes 3145736 | tf_op jit(solution)/shard_map/ppermute | solution.py:403
  131.2 13.1 %collective-permute-start.1 = (f32[32,4096]{1,0:T(8,128)S(1)}, f32[32,4096]{1,0:T(8,128)S(1)}, u32[]{:S(2)}, u32[]{:S(2)}) collective-permute-start(f32[32,4096]{1,0:T(8,128)S(1)} %get-tuple-element.26), channel_id=1, source_target_pairs={{0,64},{4,68},{8,72},{12,76},{16,80},{20,84},{24,88},{28,92},{32,9... | collective-permute-start | bytes 1572872 | tf_op jit(solution)/shard_map/ppermute | solution.py:403
  136.6 91.5 %all-to-all-start.1 = ((bf16[8,16,4608]{2,1,0:T(8,128)(2,1)}), bf16[8,16,4608]{2,1,0:T(8,128)(2,1)S(1)}, u32[]{:S(2)}, u32[]{:S(2)}) async-start(bf16[8,16,4608]{2,1,0:T(8,128)(2,1)} %bitcast.14), calls=%async_computation.1 | async-start | bytes 2359296 | tf_op jit(solution)/shard_map/all_to_all | solution.py:438
  224.9 9.7 %collective-permute-start.2 = (f32[16,4096]{1,0:T(8,128)S(1)}, f32[16,4096]{1,0:T(8,128)S(1)}, u32[]{:S(2)}, u32[]{:S(2)}) collective-permute-start(f32[16,4096]{1,0:T(8,128)S(1)} %get-tuple-element.28), channel_id=1, source_target_pairs={{0,128},{4,132},{8,136},{12,140},{16,144},{20,148},{24,152},{28,15... | collective-permute-start | bytes 786440 | tf_op jit(solution)/shard_map/ppermute | solution.py:403
  238.4 23.9 %copy-start.2 = (s32[512]{0:T(512)S(1)}, s32[512]{0:T(512)}, u32[]{:S(2)}) copy-start(s32[512]{0:T(512)} %param.10) | copy-start | bytes 6148
  277.4 0.7 copy-start.3

commit v4 on v2

--- a/solution.py
+++ b/solution.py
@@ -183,20 +183,83 @@
     )(*ins)
 
 
-def factor_kernel(level, *refs):
-    pivots, coupled = refs[:2]
-    out, w = refs[-2:]
+def level_kernel(level, *refs):
+    last = level == 2
+    ysize = 1 << level
+    piece, coupled, upd = refs[:3]
+    order = refs[3] if last else None
+    outs, scratch = refs[3 + last:5 + last], refs[5 + last:]
+    own_out, second_out = outs
+    a, w, fi, fj, prod, got, upd_in, send_sem, recv_sem = scratch
     r = coupled.shape[0]
+    half = prod.shape[2]
     n = K
+    cube_at = lax.axis_index("cube")
+    zh = lax.axis_index("panel")
+    place = lax.rem(cube_at, 8)
+    core = lax.rem(cube_at, 2)
+    x = lax.rem(cube_at // 2, 4)
+    zl = lax.rem(cube_at // 8, 2)
+    yfull = cube_at // 16
+    y = lax.rem(yfull, ysize)
+    ybase = yfull - y
+    mine = (y * 2 + zl) * PANELS + zh
+
+    def target(y, zl, w, zh):
+        return {"cube": (ybase + y) * 16 + zl * 8 + w, "panel": zh}
+
+    def turned(a, b, c):
+        return target(lax.rem(y + a, ysize), lax.rem(zl + b, 2), place, lax.rem(zh + c, 4))
+
+    z_peers = [turned(0, b, c) for b in range(2) for c in range(4) if b + c]
+    v_peers = z_peers + [turned(d, b, c) for d in range(1, ysize) for b in range(2) for c in range(4)]
+    w_places = [lax.rem(place + d, 8) for d in range(1, 8)]
+    w_peers = [target(y, zl, q, zh) for q in w_places]
+    cross_places, cross_peers = [], []
+    if not last:
+        bit = 1 << level
+        across = yfull + bit - 2 * bit * lax.rem(yfull // bit, 2)
+        cross_places = [place] + w_places
+        cross_peers = [{"cube": across * 16 + zl * 8 + q, "panel": zh} for q in cross_places]
+    everyone = v_peers + w_peers + cross_peers
+    barrier = pltpu.get_barrier_semaphore()
+    for peer in everyone:
+        pl.semaphore_signal(barrier, inc=1, device_id=peer, device_id_type=pl.DeviceIdType.MESH)
+    a[pl.ds(y, 1), pl.ds(zl, 1), pl.ds(x, 1), pl.ds(core, 1), pl.ds(zh, 1)] = piece[...][None, None, None, None, None]
+    pl.semaphore_wait(barrier, len(everyone))
+    copies = []
+
+    def send(src, dst, peer):
+        copy = pltpu.make_async_remote_copy(
+            src_ref=src, dst_ref=dst, send_sem=send_sem.at[len(copies)], recv_sem=recv_sem.at[len(copies)],
+            device_id=peer, device_id_type=pl.DeviceIdType.MESH,
+        )
+        copy.start()
+        copies.append(copy)
+        return copy
+
+    early = None
+    stages = [
+        (z_peers, a.at[y, zl, x, core, zh]),
+        ([target(y, zl, lax.rem(x + d, 4) * 2 + core, zh) for d in range(1, 4)], a.at[y, :, x, core]),
+        ([turned(d, 0, 0) for d in range(1, ysize)], a.at[y, :, :, core]),
+        ([target(y, zl, x * 2 + 1 - core, zh)], a.at[:, :, :, core]),
+    ]
+    for number, (peers, part) in enumerate(stages):
+        started = [send(part, part, peer) for peer in peers]
+        if number == 0 and not last:
+            early = send(upd.at[half:], upd_in, cross_peers[0])
+        for copy in started:
+            copy.wait_recv()
+
+    flat = a.reshape(4 * n, 128)
     ct = coupled[...]
-    if level == 2:
-        order = refs[2]
+    if last:
         move = (lax.broadcasted_iota(i32, (n, n), 0) == order[...]).astype(f32).astype(bf16)
         ch, cl = split(ct)
         ct = jnp.dot(ch, move, preferred_element_type=f32) + jnp.dot(cl, move, preferred_element_type=f32)
-        a = jnp.concatenate([pivots[pl.ds(c, n, stride=4), :] for c in range(4)], axis=1)
-        ah, al = split(a)
-        for part, source in enumerate((ah, al)):
+        full = jnp.concatenate([flat[pl.ds(c, n, stride=4), :] for c in range(4)], axis=1)
+        for part, source in enumerate(split(full)):
             cols = jnp.dot(source, move, preferred_element_type=f32).astype(bf16)
             both = lax.dot_general(move, cols, (((0,), (0,)), ((), ())), preferred_element_type=f32)
             if part == 0:
@@ -205,11 +268,19 @@
                 w[:, :n] += both
     else:
         for c in range(4):
-            w[:, c * 128:(c + 1) * 128] = pivots[pl.ds(c, n, stride=4), :]
+            w[:, c * 128:(c + 1) * 128] = flat[pl.ds(c, n, stride=4), :]
     if r < 128:
         ct = jnp.concatenate([ct, jnp.zeros((128 - r, n), f32)], axis=0)
     w[:, n:] = ct.T
     blocks = n // 128
+    factors = [[], []]
+
+    def spread(lo, hi, group):
+        for peer in v_peers:
+            group.append(send(fj.at[lo:hi, mine], fj.at[lo:hi, mine], peer))
+        for peer in w_peers:
+            group.append(send(fi.at[lo:hi, place], fi.at[lo:hi, place], peer))
+
     for b in range(blocks):
         lo = b * 128
         rows = [w[lo + 8 * p: lo + 8 * p + 8, lo:lo + 128] for p in range(16)]
@@ -220,100 +291,78 @@
             w[later * 128:(later + 1) * 128, later * 128:] -= mm(
                 solved[:, off:off + 128], solved[:, off:], ((0,), (0,))
             )
-        out[:, lo:lo + 128] = solved[:, n - lo - 128:].T[:r].astype(bf16)
-
-
-def make_factor(level, pivots, coupled, order):
+        f = solved[:, n - lo - 128:].T[:r].astype(bf16)
+        if last:
+            second_out[:, lo:lo + 128] = f
+        fi[b, pl.ds(place, 1)] = f[None]
+        fj[b, pl.ds(mine, 1)] = f[None]
+        if b == blocks - 2:
+            spread(0, blocks - 1, factors[0])
+        if b == blocks - 1:
+            spread(blocks - 1, blocks, factors[1])
+
+    def block_product(lo, hi):
+        left = jnp.concatenate([fi[b].reshape(8 * r, 128) for b in range(lo, hi)], axis=1)
+        right = jnp.concatenate([fj[b].reshape(512, 128) for b in range(lo, hi)], axis=1)
+        return lax.dot_general(left, right, (((1,), (1,)), ((), ())), preferred_element_type=f32)
+
+    for copy in factors[0]:
+        copy.wait_recv()
+    product = block_product(0, blocks - 1)
+    for copy in factors[1]:
+        copy.wait_recv()
+    product = (product + block_product(blocks - 1, blocks)).reshape(8, r, 512)
+    for part in range(r // half):
+        prod[part] = product[:, part * half:(part + 1) * half]
+    back = [send(prod.at[0, q], got.at[0, place], peer) for q, peer in zip(w_places, w_peers)]
+    back += [send(prod.at[1, q], got.at[1, place], peer) for q, peer in zip(cross_places, cross_peers)]
+    got[0, pl.ds(place, 1)] = prod[0, pl.ds(place, 1)]
+    if early is not None:
+        early.wait_recv()
+    for copy in back:
+        copy.wait_recv()
+    wide = PANELS * r
+    for part in range(r // half):
+        source = upd_in if part else upd
+        out = second_out if part else own_out
+        for block in range(2 * ysize):
+            parts = [got[part, q, :, block * wide:(block + 1) * wide] for q in range(8)]
+            lo = block * 8 * wide
+            out[:, lo:lo + 8 * wide] = source[:half, lo:lo + 8 * wide] - jnp.concatenate(parts, axis=1)
+    for copy in copies:
+        copy.wait_send()
+
+
+def eliminate(level, piece, coupled, update_rows, order):
+    last = level == 2
+    ysize = 1 << level
     r = coupled.shape[0]
-    ins = (pivots, coupled) + ((order,) if level == 2 else ())
+    half = r if last else r // 2
+    ins = (piece, coupled, update_rows) + ((order,) if last else ())
+    second = jax.ShapeDtypeStruct((r, K), bf16) if last else jax.ShapeDtypeStruct((half, U), f32)
+    v = 8 * ysize
+    count = 7 + 3 + ysize - 1 + 1 + 2 * (v - 1 + 7) + 7 + (0 if last else 9)
     return pl.pallas_call(
-        functools.partial(factor_kernel, level),
-        out_shape=jax.ShapeDtypeStruct((r, K), bf16),
+        functools.partial(level_kernel, level),
+        out_shape=(jax.ShapeDtypeStruct((half, U), f32), second),
         in_specs=[VMEM] * len(ins),
-        out_specs=VMEM,
-        scratch_shapes=[pltpu.VMEM((K, K + 128), f32)],
-        compiler_params=pltpu.CompilerParams(vmem_limit_bytes=32 * 2**20),
-        cost_estimate=pl.CostEstimate(flops=10**10, bytes_accessed=40 * 10**6, transcendentals=0),
-        name="factor%d" % level,
-    )(*ins)
-
-
-def gather_kernel(ysize, x_ref, out, send_sem, recv_sem, local_sem):
-    cube_at = lax.axis_index("cube")
-    zh = lax.axis_index("panel")
-    core = lax.rem(cube_at, 2)
-    x = lax.rem(cube_at // 2, 4)
-    zl = lax.rem(cube_at // 8, 2)
-    yfull = cube_at // 16
-    y = lax.rem(yfull, ysize)
-    ybase = yfull - y
-
-    def target(y, zl, x, core, zh):
-        return {"cube": (ybase + y) * 16 + zl * 8 + x * 2 + core, "panel": zh}
-
-    def shifted(v, d, size):
-        return lax.rem(v + d, size)
-
-    z_peers = [
-        target(y, shifted(zl, a, 2), x, core, shifted(zh, b, 4))
-        for a in range(2) for b in range(4) if a + b
-    ]
-    x_peers = [target(y, zl, shifted(x, d, 4), core, zh) for d in range(1, 4)]
-    y_peers = [target(shifted(y, d, ysize), zl, x, core, zh) for d in range(1, ysize)]
-    core_peers = [target(y, zl, x, 1 - core, zh)]
-    stages = [
-        (z_peers, out.at[y, zl, x, core, zh]),
-        (x_peers, out.at[y, :, x, core]),
-        (y_peers, out.at[y, :, :, core]),
-        (core_peers, out.at[:, :, :, core]),
-    ]
-    everyone = z_peers + x_peers + y_peers + core_peers
-    keep = pltpu.make_async_copy(x_ref, out.at[y, zl, x, core, zh], local_sem)
-    keep.start()
-    barrier = pltpu.get_barrier_semaphore()
-    for peer in everyone:
-        pl.semaphore_signal(barrier, inc=1, device_id=peer, device_id_type=pl.DeviceIdType.MESH)
-    pl.semaphore_wait(barrier, len(everyone))
-    keep.wait()
-    number = 0
-    sent = []
-    for peers, part in stages:
-        copies = []
-        for peer in peers:
-            copies.append(pltpu.make_async_remote_copy(
-                src_ref=part, dst_ref=part, send_sem=send_sem.at[number], recv_sem=recv_sem.at[number],
-                device_id=peer, device_id_type=pl.DeviceIdType.MESH,
-            ))
-            number += 1
-        for copy in copies:
-            copy.start()
-        for copy in copies:
-            copy.wait_recv()
-        sent += copies
-    for copy in sent:
-        copy.wait_send()
-
-
-def gather(level, piece, ident):
-    ysize = 1 << level
-    rows, cols = piece.shape
-    count = 7 + 3 + ysize - 1 + 1
-    out = pl.pallas_call(
-        functools.partial(gather_kernel, ysize),
-        out_shape=jax.ShapeDtypeStruct((ysize, 2, 4, 2, 4, rows, cols), piece.dtype),
-        in_specs=[VMEM],
-        out_specs=VMEM,
+        out_specs=(VMEM, VMEM),
         scratch_shapes=[
+            pltpu.VMEM((ysize, 2, 4, 2, 4) + piece.shape, f32),
+            pltpu.VMEM((K, K + 128), f32),
+            pltpu.VMEM((4, 8, r, 128), bf16),
+            pltpu.VMEM((4, v, r, 128), bf16),
+            pltpu.VMEM((r // half, 8, half, 512), f32),
+            pltpu.VMEM((r // half, 8, half, 512), f32),
+            pltpu.VMEM((half, U), f32),
             pltpu.SemaphoreType.DMA((count,)), pltpu.SemaphoreType.DMA((count,)),
-            pltpu.SemaphoreType.DMA(()),
         ],
         compiler_params=pltpu.CompilerParams(
-            collective_id=ident, has_side_effects=True, vmem_limit_bytes=32 * 2**20
+            collective_id=level, has_side_effects=True, vmem_limit_bytes=40 * 2**20
         ),
-        cost_estimate=pl.CostEstimate(flops=10**10, bytes_accessed=60 * 10**6, transcendentals=0),
-        name="gather%d" % ident,
-    )(piece)
-    return out.reshape(-1, cols)
+        cost_estimate=pl.CostEstimate(flops=3 * 10**10, bytes_accessed=150 * 10**6, transcendentals=0),
+        name="level%d" % level,
+    )(*ins)
 
 
 def from_partner(shard, stride):
@@ -358,27 +407,20 @@
 def body(leaf_updates, extend_maps, front_diagonal, pivot_order, coupling_rows, coupling_owner, coupling_slot):
     routed = route_plane(coupling_rows, coupling_owner, coupling_slot)
     assembly = None
-    children = leaf_updates
+    r = leaf_updates.shape[0] // 2
+    own, incoming = leaf_updates[:r], from_partner(leaf_updates[r:], 3)
     order = pivot_order.reshape(1, K)
     for level in range(3):
-        r = children.shape[0] // 2
-        incoming = from_partner(children[r:], 3 + level)
         if level == 2:
             assembly = jnp.sum(routed.astype(f32), axis=0)
         piece, coupled, update_rows = assemble(
-            level, extend_maps, front_diagonal, children[:r], incoming, assembly
+            level, extend_maps, front_diagonal, own, incoming, assembly
         )
-        pivots = gather(level, piece, 2 * level)
-        factor = make_factor(level, pivots, coupled, order)
+        own, incoming = eliminate(level, piece, coupled, update_rows, order)
         if level == 0:
-            routed, factor = lax.optimization_barrier((routed, factor))
+            routed, own = lax.optimization_barrier((routed, own))
             routed = route_column(routed)
-        collected = gather(level, factor, 2 * level + 1)
-        product = lax.dot_general(
-            factor, collected, (((1,), (1,)), ((), ())), preferred_element_type=f32
-        )
-        children = update_rows - product
-    return (factor, children)
+    return (incoming, own)
 
 
 def solution(mesh):

time: 371 us -> 291 us (0.78)
  Pallas kernels: 295 us -> 236 us
  waiting for transfers between devices: 35.6 us -> 23.3 us
  matrix products: 13.7 us -> 9.85 us
    pallas_call x9 -> x3, Pallas kernels: 283 us -> 224 us  [eliminate(): pl.pallas_call(functools.partial(level_kernel, level), out_shape=(jax.Sha...]
    ppermute x3 -> x1, waiting for transfers between devices: 35.6 us -> 23.3 us  [from_partner(): lax.ppermute(shard, 'cube', [(i, i ^ 1 << stride) for i in range(64)])]
    dot_general x3 -> x0, matrix products: 3.87 us -> none  [body(): lax.dot_general(factor, collected, (((1,), (1,)), ((), ())), preferred_el...]
  transfers between devices with their start and end apart: 5 -> 3, of which waited for: 3 -> 1; matrix products, arithmetic and copies ran while one was open for 2% -> 0% of each run, Pallas kernels for 44% -> 60%
where the time goes in v4:
time: 291 us; the launch traced here: 288 us
  Pallas kernels  236 us (81%)
  waiting for transfers between devices  23.3 us (8%)
  starting transfers between devices  14.6 us (5%)
  matrix products  9.85 us (3%)
    pallas_call x3, Pallas kernels, eliminate(): pl.pallas_call(functools.partial(level_kernel, level), out_shape=(jax.Sha...  224 us
    ppermute x1, waiting for transfers between devices, from_partner(): lax.ppermute(shard, 'cube', [(i, i ^ 1 << stride) for i in range(64)])  23.3 us
    pallas_call x3, Pallas kernels, assemble(): pl.pallas_call(functools.partial(assemble_kernel, level), out_shape=(jax....  12.2 us
    all_to_all x1, starting transfers between devices, route_plane(): lax.all_to_all(outgoing, 'cube', 0, 0, axis_index_groups=groups, tiled=True)  8.77 us
  transfers between devices with their start and end apart: 3, of which 1 were waited for; matrix products, arithmetic and copies ran while one was open for 0% of the time, Pallas kernels for 60%

profile of v4, /device:TPU:1, one launch (start us, length us, event | category | flops | bytes accessed | tf_op | source)
XLA Modules:
  0.0 288.1 jit_solution(16772846300851335504)
XLA Ops:
  0.6 0.7 fusion.10
  1.3 0.2 fusion.4
  1.5 0.7 convert_add_fusion
  2.3 0.1 fusion.7
  2.4 5.4 %convolution_convert_fusion = bf16[512,4736]{1,0:T(8,128)(2,1)} fusion(bf16[256,128]{1,0:T(8,128)(2,1)S(1)} %fusion.7, bf16[256,4608]{1,0:T(8,128)(2,1)} %param.11, s32[256]{0:T(256)S(1)} %get-tuple-element.38), kind=kOutput, calls=%fused_computation | convolution fusion | flops 1248919552 | bytes 7275520 | tf_op jit(solution)/shard_map/dot_general | solution.py:389
  7.7 8.8 %all-to-all-start = ((bf16[32,16,4736]{2,1,0:T(8,128)(2,1)}), bf16[32,16,4736]{2,1,0:T(8,128)(2,1)}, u32[]{:S(2)}, u32[]{:S(2)}) async-start(bf16[32,16,4736]{2,1,0:T(8,128)(2,1)} %bitcast.7), calls=%async_computation | async-start | bytes 9699328 | tf_op jit(solution)/shard_map/all_to_all | solution.py:392
  16.5 0.0 copy-start
  16.5 0.0 copy-start.1
  16.6 0.2 fusion.15
  16.7 2.2 collective-permute-start
  19.0 23.3 %collective-permute-done.refs_3_ = f32[64,4096]{1,0:T(8,128)S(1)} collective-permute-done((f32[64,4096]{1,0:T(8,128)S(1)}, f32[64,4096]{1,0:T(8,128)S(1)}, u32[]{:S(2)}, u32[]{:S(2)}) %collective-permute-start) | collective-permute-done | bytes 1048608 | tf_op jit(solution)/shard_map/ppermute | solution.py:369
  42.3 4.4 %assemble0.1 = (f32[32,128]{1,0:T(8,128)S(1)}, f32[64,512]{1,0:T(8,128)S(1)}, f32[64,4096]{1,0:T(8,128)S(1)}) custom-call(s32[14,4096]{1,0:T(8,128)S(1)} %copy-done, f32[7,4608]{1,0:T(8,128)S(1)} %copy-done.1, f32[64,4096]{1,0:T(8,128)S(1)} %get-tuple-element.37.refs_2_, f32[64,4096]{1,0:T(8,128)S(1)} %collective-permute-done.refs_3_), custom_call_target="tpu_custom_call" | custom-call | flops 2000000000 | bytes 4000000 | tf_op jit(solution)/shard_map/assemble0/pallas_call | solution.py:170
  46.7 84.4 %level0.1 = (f32[32,4096]{1,0:T(8,128)S(1)}, f32[32,4096]{1,0:T(8,128)S(1)}) custom-call(f32[32,128]{1,0:T(8,128)S(1)} %get-tuple-element.19.refs_0_, f32[64,512]{1,0:T(8,128)S(1)} %get-tuple-element.20.refs_1_, f32[64,4096]{1,0:T(8,128)S(1)} %get-tuple-element.21.refs_2_), custom_call_target="tpu_custom_call" | custom-call | flops 30000001024 | bytes 150000000 | tf_op jit(solution)/shard_map/level0/pallas_call | solution.py:345
  131.1 0.0 all-to-all-done
  131.1 4.3 %convolution_convert_fusion.1 = bf16[128,4608]{1,0:T(8,128)(2,1)} fusion(bf16[512,4736]{1,0:T(8,128)(2,1)} %bitcast.3), kind=kOutput, calls=%fused_computation.1 | convolution fusion | flops 604569600 | bytes 6029312 | tf_op jit(solution)/shard_map/dot_general | solution.py:397
  135.3 3.6 %all-to-all-start.1 = ((bf16[8,16,4608]{2,1,0:T(8,128)(2,1)}), bf16[8,16,4608]{2,1,0:T(8,128)(2,1)S(1)}, u32[]{:S(2)}, u32[]{:S(2)}) async-start(bf16[8,16,4608]{2,1,0:T(8,128)(2,1)} %bitcast.8), calls=%async_computation.1 | async-start | bytes 2359296 | tf_op jit(solution)/shard_map/all_to_all | solution.py:404
  138.9 4.0 %assemble1.1 = (f32[16,128]{1,0:T(8,128)S(1)}, f32[32,512]{1,0:T(8,128)S(1)}, f32[32,4096]{1,0:T(8,128)S(1)}) custom-call(s32[14,4096]{1,0:T(8,128)S(1)} %copy-done, f32[7,4608]{1,0:T(8,128)S(1)} %copy-done.1, f32[32,4096]{1,0:T(8,128)S(1)} %get-tuple-element.23.refs_2_, f32[32,4096]{1,0:T(8,128)S(1)} %get-tuple-element.24.refs_3_), custom_call_target="tpu_custom_call" | custom-call | flops 2000000000 | bytes 4000000 | tf_op jit(solution)/shard_map/assemble1/pallas_call | solution.py:170
  143.0 80.6 %level1.1 = (f32[16,4096]{1,0:T(8,128)S(1)}, f32[16,4096]{1,0:T(8,128)S(1)}) custom-call(f32[16,128]{1,0:T(8,128)S(1)} %get-tuple-element.25.refs_0_, f32[32,512]{1,0:T(8,128)S(1)} %get-tuple-element.26.refs_1_, f32[32,4096]{1,0:T(8,128)S(1)} %get-tuple-element.27.refs_2_), custom_call_target="tpu_custom_call" | custom-call | flops 30000001024 | bytes 150000000 | tf_op jit(solution)/shard_map/level1/pallas_call | solution.py:345
  223.6 0.2 convert_reduce_fusion.refs_4_
  223.8 0.0 copy-start.2
  223.8 3.8 %assemble2.1 = (f32[8,128]{1,0:T(8,128)S(1)}, f32[16,512]{1,0:T(8,128)S(1)}, f32[16,4096]{1,0:T(8,128)S(1)}) custom-call(s32[14,4096]{1,0:T(8,128)S(1)} %copy-done, f32[7,4608]{1,0:T(8,128)S(1)} %copy-done.1, f32[16,4096]{1,0:T(8,128)S(1)} %get-tuple-element.28.refs_2_, f32[16,4096]{1,0:T(8,128)S(1)} %get-tuple-element.29.refs_3_, ...), custom_call_target="tpu_custom_call" | custom-call | flops 2000000000 | bytes 4000000 | tf_op jit(solution)/shard_map/assemble2/pallas_call | solution.py:170
  227.6 58.9 %level2.1 = (f32[16,4096]{1,0:T(8,128)S(1)}, bf16[16,512]{1,0:T(8,128)(2,1)S(1)}) custom-call(f32[8,128]{1,0:T(8,128)S(1)} %get-tuple-element.31.refs_0_, f32[16,512]{1,0:T(8,128)S(1)} %get-tuple-element.32.refs_1_, f32[16,4096]{1,0:T(8,128)S(1)} %get-tuple-element.33.refs_2_, s32[1,512]{1,0:T(1,128)S(1)} %bitcast.6), custom_call_target="tpu_custom_call" | custom-call | flops 30000001024 | bytes 150000000 | tf_op jit(solution)/shard_map/level2/pallas_call | solution.py:345
  286.5 0.6 copy.11
  287.1 0.7 copy.12
  (6 shorter events, 0.0 us)
Async XLA Ops:
  7.7 8.8 %copy-start.3 = (f32[128,4096]{1,0:T(8,128)S(1)}, f32[128,4096]{1,0:T(8,128)}, u32[]{:S(2)}) copy-start(f32[128,4096]{1,0:T(8,128)} %param.7) | copy-start | bytes 6291460
  7.7 123.3 %all-to-all-start = ((bf16[32,16,4736]{2,1,0:T(8,128)(2,1)}), bf16[32,16,4736]{2,1,0:T(8,128)(2,1)}, u32[]{:S(2)}, u32[]{:S(2)}) async-start(bf16[32,16,4736]{2,1,0:T(8,128)(2,1)} %bitcast.7), calls=%async_computation | async-start | bytes 9699328 | tf_op jit(solution)/shard_map/all_to_all | solution.py:392
  16.5 25.8 %copy-start = (s32[14,4096]{1,0:T(8,128)S(1)}, s32[14,4096]{1,0:T(8,128)}, u32[]{:S(2)}) copy-start(s32[14,4096]{1,0:T(8,128)} %refs_0_.5) | copy-start | bytes 688132
  16.5 25.8 %copy-start.1 = (f32[7,4608]{1,0:T(8,128)S(1)}, f32[7,4608]{1,0:T(8,128)}, u32[]{:S(2)}) copy-start(f32[7,4608]{1,0:T(8,128)} %refs_1_.5) | copy-start | bytes 387076
  16.7 25.5 %collective-permute-start = (f32[64,4096]{1,0:T(8,128)S(1)}, f32[64,4096]{1,0:T(8,128)S(1)}, u32[]{:S(2)}, u32[]{:S(2)}) collective-permute-start(f32[64,4096]{1,0:T(8,128)S(1)} %get-tuple-element.36), channel_id=1, source_target_pairs={{0,32},{4,36},{8,40},{12,44},{16,48},{20,52},{24,56},{28,60},{32,0... | collective-permute-start | bytes 3145736 | tf_op jit(solution)/shard_map/ppermute | solution.py:369
  135.3 88.3 %all-to-all-start.1 = ((bf16[8,16,4608]{2,1,0:T(8,128)(2,1)}), bf16[8,16,4608]{2,1,0:T(8,128)(2,1)S(1)}, u32[]{:S(2)}, u32[]{:S(2)}) async-start(bf16[8,16,4608]{2,1,0:T(8,128)(2,1)} %bitcast.8), calls=%async_computation.1 | async-start | bytes 2359296 | tf_op jit(solution)/shard_map/all_to_all | solution.py:404
  223.8 3.8 %copy-start.2 = (s32[512]{0:T(512)S(1)}, s32[512]{0:T(512)}, u32[]{:S(2)}) copy-start(s32[512]{0:T(512)} %param.10) | copy-start | bytes 6148

commit v5 on v4

--- a/solution.py
+++ b/solution.py
@@ -124,7 +124,7 @@
         xs, ss = [], []
         for which, ref in enumerate((mine, other)):
             x = ref[:, c * 256:(c + 1) * 256]
-            hi, lo = split(x)
+            hi, lo = (x, jnp.zeros_like(x)) if x.dtype == bf16 else split(x)
             pick = lambda y: jnp.dot(sel[which], y, preferred_element_type=f32).astype(bf16)
             xs.append(jnp.concatenate([pick(hi), pick(lo)], axis=0))
             m = map_row[which:which + 1, c * 256:(c + 1) * 256]
@@ -226,6 +226,14 @@
     for peer in everyone:
         pl.semaphore_signal(barrier, inc=1, device_id=peer, device_id_type=pl.DeviceIdType.MESH)
     a[pl.ds(y, 1), pl.ds(zl, 1), pl.ds(x, 1), pl.ds(core, 1), pl.ds(zh, 1)] = piece[...][None, None, None, None, None]
+    own = coupled[...]
+    if last:
+        move = (lax.broadcasted_iota(i32, (n, n), 0) == order[...]).astype(f32).astype(bf16)
+        ch, cl = split(own)
+        own = jnp.dot(ch, move, preferred_element_type=f32) + jnp.dot(cl, move, preferred_element_type=f32)
+    own_rows = own.astype(bf16)[None]
+    fi[pl.ds(place, 1)] = own_rows
+    fj[pl.ds(mine, 1)] = own_rows
     pl.semaphore_wait(barrier, len(everyone))
     copies = []
 
@@ -245,19 +253,20 @@
         ([turned(d, 0, 0) for d in range(1, ysize)], a.at[y, :, :, core]),
         ([target(y, zl, x * 2 + 1 - core, zh)], a.at[:, :, :, core]),
     ]
+    gathered = []
     for number, (peers, part) in enumerate(stages):
         started = [send(part, part, peer) for peer in peers]
         if number == 0 and not last:
             early = send(upd.at[half:], upd_in, cross_peers[0])
+        if number == 1:
+            gathered += [send(fj.at[mine], fj.at[mine], peer) for peer in v_peers]
+        if number == 2:
+            gathered += [send(fi.at[place], fi.at[place], peer) for peer in w_peers]
         for copy in started:
             copy.wait_recv()
 
     flat = a.reshape(4 * n, 128)
-    ct = coupled[...]
     if last:
-        move = (lax.broadcasted_iota(i32, (n, n), 0) == order[...]).astype(f32).astype(bf16)
-        ch, cl = split(ct)
-        ct = jnp.dot(ch, move, preferred_element_type=f32) + jnp.dot(cl, move, preferred_element_type=f32)
         full = jnp.concatenate([flat[pl.ds(c, n, stride=4), :] for c in range(4)], axis=1)
         for part, source in enumerate(split(full)):
             cols = jnp.dot(source, move, preferred_element_type=f32).astype(bf16)
@@ -266,52 +275,52 @@
                 w[:, :n] = both
             else:
                 w[:, :n] += both
+        w[:, n:] = jnp.concatenate([own, jnp.zeros((128 - r, n), f32)], axis=0).T
     else:
         for c in range(4):
             w[:, c * 128:(c + 1) * 128] = flat[pl.ds(c, n, stride=4), :]
-    if r < 128:
-        ct = jnp.concatenate([ct, jnp.zeros((128 - r, n), f32)], axis=0)
-    w[:, n:] = ct.T
     blocks = n // 128
-    factors = [[], []]
-
-    def spread(lo, hi, group):
-        for peer in v_peers:
-            group.append(send(fj.at[lo:hi, mine], fj.at[lo:hi, mine], peer))
-        for peer in w_peers:
-            group.append(send(fi.at[lo:hi, place], fi.at[lo:hi, place], peer))
-
+    width = w.shape[1]
+    first, second = ((0,), (0,)), ((1,), (0,))
     for b in range(blocks):
-        lo = b * 128
-        rows = [w[lo + 8 * p: lo + 8 * p + 8, lo:lo + 128] for p in range(16)]
+        lo, hi = b * 128, b * 128 + 128
+        rows = [w[lo + 8 * p: lo + 8 * p + 8, lo:hi] for p in range(16)]
         inverse = jnp.concatenate(diag_inverse(rows), axis=0)
-        solved = mm(inverse, w[lo:lo + 128, lo + 128:], ((1,), (0,)))
+        if hi < width:
+            solved = mm(inverse, w[lo:hi, hi:], second)
         for later in range(b + 1, blocks):
             off = (later - b - 1) * 128
-            w[later * 128:(later + 1) * 128, later * 128:] -= mm(
-                solved[:, off:off + 128], solved[:, off:], ((0,), (0,))
-            )
-        f = solved[:, n - lo - 128:].T[:r].astype(bf16)
+            w[later * 128:later * 128 + 128, later * 128:] -= mm(solved[:, off:off + 128], solved[:, off:], first)
         if last:
-            second_out[:, lo:lo + 128] = f
-        fi[b, pl.ds(place, 1)] = f[None]
-        fj[b, pl.ds(mine, 1)] = f[None]
-        if b == blocks - 2:
-            spread(0, blocks - 1, factors[0])
-        if b == blocks - 1:
-            spread(blocks - 1, blocks, factors[1])
-
-    def block_product(lo, hi):
-        left = jnp.concatenate([fi[b].reshape(8 * r, 128) for b in range(lo, hi)], axis=1)
-        right = jnp.concatenate([fj[b].reshape(512, 128) for b in range(lo, hi)], axis=1)
-        return lax.dot_general(left, right, (((1,), (1,)), ((), ())), preferred_element_type=f32)
-
-    for copy in factors[0]:
+            second_out[:, lo:hi] = solved[:, n - hi:].T[:r].astype(bf16)
+        done = inverse
+        if b:
+            done = jnp.concatenate([mm(inverse, w[lo:hi, :lo], second), inverse], axis=1)
+            w[lo:hi, :lo] = done[:, :lo]
+        w[lo:hi, lo:hi] = inverse
+        for later in range(b + 1, blocks):
+            off = (later - b - 1) * 128
+            part = mm(solved[:, off:off + 128], done, first)
+            if b:
+                w[later * 128:later * 128 + 128, :lo] -= part[:, :lo]
+            w[later * 128:later * 128 + 128, lo:hi] = -part[:, lo:]
+
+    for copy in gathered:
         copy.wait_recv()
-    product = block_product(0, blocks - 1)
-    for copy in factors[1]:
-        copy.wait_recv()
-    product = (product + block_product(blocks - 1, blocks)).reshape(8, r, 512)
+    both = jnp.concatenate([fi[...].reshape(8 * r, n), fj[...].reshape(512, n)], axis=0)
+    across_rows = ((1,), (1,))
+    factors = []
+    for b in range(blocks):
+        hi = b * 128 + 128
+        parts = [
+            lax.dot_general(both[:, :hi], part, (across_rows, ((), ())), preferred_element_type=f32)
+            for part in split(w[hi - 128:hi, :hi])
+        ]
+        factors.append((parts[0] + parts[1]).astype(bf16))
+    factors = jnp.concatenate(factors, axis=1)
+    product = lax.dot_general(
+        factors[:8 * r], factors[8 * r:], (across_rows, ((), ())), preferred_element_type=f32
+    ).astype(bf16).reshape(8, r, 512)
     for part in range(r // half):
         prod[part] = product[:, part * half:(part + 1) * half]
     back = [send(prod.at[0, q], got.at[0, place], peer) for q, peer in zip(w_places, w_peers)]
@@ -326,7 +335,7 @@
         source = upd_in if part else upd
         out = second_out if part else own_out
         for block in range(2 * ysize):
-            parts = [got[part, q, :, block * wide:(block + 1) * wide] for q in range(8)]
+            parts = [got[part, q, :, block * wide:(block + 1) * wide].astype(f32) for q in range(8)]
             lo = block * 8 * wide
             out[:, lo:lo + 8 * wide] = source[:half, lo:lo + 8 * wide] - jnp.concatenate(parts, axis=1)
     for copy in copies:
@@ -341,7 +350,7 @@
     ins = (piece, coupled, update_rows) + ((order,) if last else ())
     second = jax.ShapeDtypeStruct((r, K), bf16) if last else jax.ShapeDtypeStruct((half, U), f32)
     v = 8 * ysize
-    count = 7 + 3 + ysize - 1 + 1 + 2 * (v - 1 + 7) + 7 + (0 if last else 9)
+    count = 7 + 3 + ysize - 1 + 1 + (v - 1 + 7) + 7 + (0 if last else 9)
     return pl.pallas_call(
         functools.partial(level_kernel, level),
         out_shape=(jax.ShapeDtypeStruct((half, U), f32), second),
@@ -349,11 +358,11 @@
         out_specs=(VMEM, VMEM),
         scratch_shapes=[
             pltpu.VMEM((ysize, 2, 4, 2, 4) + piece.shape, f32),
-            pltpu.VMEM((K, K + 128), f32),
-            pltpu.VMEM((4, 8, r, 128), bf16),
-            pltpu.VMEM((4, v, r, 128), bf16),
-            pltpu.VMEM((r // half, 8, half, 512), f32),
-            pltpu.VMEM((r // half, 8, half, 512), f32),
+            pltpu.VMEM((K, K + (128 if last else 0)), f32),
+            pltpu.VMEM((8, r, K), bf16),
+            pltpu.VMEM((v, r, K), bf16),
+            pltpu.VMEM((r // half, 8, half, 512), bf16),
+            pltpu.VMEM((r // half, 8, half, 512), bf16),
             pltpu.VMEM((half, U), f32),
             pltpu.SemaphoreType.DMA((count,)), pltpu.SemaphoreType.DMA((count,)),
         ],
@@ -408,7 +417,7 @@
     routed = route_plane(coupling_rows, coupling_owner, coupling_slot)
     assembly = None
     r = leaf_updates.shape[0] // 2
-    own, incoming = leaf_updates[:r], from_partner(leaf_updates[r:], 3)
+    own, incoming = leaf_updates[:r], from_partner(leaf_updates[r:].astype(bf16), 3)
     order = pivot_order.reshape(1, K)
     for level in range(3):
         if level == 2:

time: 291 us -> 247 us (0.85)
  Pallas kernels: 236 us -> 199 us
  waiting for transfers between devices: 23.3 us -> 12 us
  starting transfers between devices: 14.6 us -> 19.2 us
    pallas_call x3, Pallas kernels: 224 us -> 188 us  [eliminate(): pl.pallas_call(functools.partial(level_kernel, level), out_shape=(jax.Sha...]
    ppermute x1, waiting for transfers between devices: 23.3 us -> 12 us  [from_partner(): lax.ppermute(shard, 'cube', [(i, i ^ 1 << stride) for i in range(64)])]
    all_to_all x1, starting transfers between devices: 3.56 us -> 8.19 us  [route_column(): lax.all_to_all(sums, ('cube', 'panel'), 0, 0, axis_index_groups=groups, t...]
  transfers between devices with their start and end apart: 3 -> 3, of which waited for: 1 -> 1; matrix products, arithmetic and copies ran while one was open for 0% -> 0% of each run, Pallas kernels for 60% -> 61%
where the time goes in v5:
time: 247 us; the launch traced here: 245 us
  Pallas kernels  199 us (81%)
  starting transfers between devices  19.2 us (8%)
  waiting for transfers between devices  12 us (5%)
  matrix products  9.84 us (4%)
    pallas_call x3, Pallas kernels, eliminate(): pl.pallas_call(functools.partial(level_kernel, level), out_shape=(jax.Sha...  188 us
    ppermute x1, waiting for transfers between devices, from_partner(): lax.ppermute(shard, 'cube', [(i, i ^ 1 << stride) for i in range(64)])  12 us
    pallas_call x3, Pallas kernels, assemble(): pl.pallas_call(functools.partial(assemble_kernel, level), out_shape=(jax....  11.7 us
    all_to_all x1, starting transfers between devices, route_plane(): lax.all_to_all(outgoing, 'cube', 0, 0, axis_index_groups=groups, tiled=True)  8.77 us
    all_to_all x1, starting transfers between devices, route_column(): lax.all_to_all(sums, ('cube', 'panel'), 0, 0, axis_index_groups=groups, t...  8.19 us
    dot_general x1, matrix products, route_plane(): outgoing = jnp.dot(choose, payload, preferred_element_type=f32).astype(bf16)  5.38 us
  transfers between devices with their start and end apart: 3, of which 1 were waited for; matrix products, arithmetic and copies ran while one was open for 0% of the time, Pallas kernels for 61%

profile of v5, /device:TPU:1, one launch (start us, length us, event | category | flops | bytes accessed | tf_op | source)
XLA Modules:
  0.0 244.7 jit_solution(15963319539940990961)
XLA Ops:
  0.6 0.7 fusion.10
  1.3 0.2 fusion.4
  1.5 0.7 convert_add_fusion
  2.3 0.1 fusion.7
  2.4 5.4 %convolution_convert_fusion = bf16[512,4736]{1,0:T(8,128)(2,1)} fusion(bf16[256,128]{1,0:T(8,128)(2,1)S(1)} %fusion.7, bf16[256,4608]{1,0:T(8,128)(2,1)} %param.11, s32[256]{0:T(256)S(1)} %get-tuple-element.36), kind=kOutput, calls=%fused_computation | convolution fusion | flops 1248919552 | bytes 7275520 | tf_op jit(solution)/shard_map/dot_general | solution.py:398
  7.7 8.8 %all-to-all-start = ((bf16[32,16,4736]{2,1,0:T(8,128)(2,1)}), bf16[32,16,4736]{2,1,0:T(8,128)(2,1)}, u32[]{:S(2)}, u32[]{:S(2)}) async-start(bf16[32,16,4736]{2,1,0:T(8,128)(2,1)} %bitcast.7), calls=%async_computation | async-start | bytes 9699328 | tf_op jit(solution)/shard_map/all_to_all | solution.py:401
  16.5 0.0 copy-start
  16.5 0.0 copy-start.1
  16.6 0.1 slice.25
  16.6 2.2 collective-permute-start
  18.9 0.1 slice.13.refs_2_
  18.9 12.0 %collective-permute-done.refs_3_ = bf16[64,4096]{1,0:T(8,128)(2,1)S(1)} collective-permute-done((bf16[64,4096]{1,0:T(8,128)(2,1)S(1)}, bf16[64,4096]{1,0:T(8,128)(2,1)S(1)}, u32[]{:S(2)}, u32[]{:S(2)}) %collective-permute-start) | collective-permute-done | bytes 524320 | tf_op jit(solution)/shard_map/ppermute | solution.py:378
  30.9 3.9 %assemble0.1 = (f32[32,128]{1,0:T(8,128)S(1)}, f32[64,512]{1,0:T(8,128)S(1)}, f32[64,4096]{1,0:T(8,128)S(1)}) custom-call(s32[14,4096]{1,0:T(8,128)S(1)} %copy-done, f32[7,4608]{1,0:T(8,128)S(1)} %copy-done.1, f32[64,4096]{1,0:T(8,128)S(1)} %slice.13.refs_2_, bf16[64,4096]{1,0:T(8,128)(2,1)S(1)} %collective-permute-done.refs_3_), custom_call_target="tpu_custom_call" | custom-call | flops 2000000000 | bytes 4000000 | tf_op jit(solution)/shard_map/assemble0/pallas_call | solution.py:170
  34.8 72.5 %level0.1 = (f32[32,4096]{1,0:T(8,128)S(1)}, f32[32,4096]{1,0:T(8,128)S(1)}) custom-call(f32[32,128]{1,0:T(8,128)S(1)} %get-tuple-element.19.refs_0_, f32[64,512]{1,0:T(8,128)S(1)} %get-tuple-element.20.refs_1_, f32[64,4096]{1,0:T(8,128)S(1)} %get-tuple-element.21.refs_2_), custom_call_target="tpu_custom_call" | custom-call | flops 30000001024 | bytes 150000000 | tf_op jit(solution)/shard_map/level0/pallas_call | solution.py:354
  107.4 4.3 %convolution_convert_fusion.1 = bf16[128,4608]{1,0:T(8,128)(2,1)} fusion(bf16[512,4736]{1,0:T(8,128)(2,1)} %bitcast.3), kind=kOutput, calls=%fused_computation.1 | convolution fusion | flops 604569600 | bytes 6029312 | tf_op jit(solution)/shard_map/dot_general | solution.py:406
  111.6 8.2 %all-to-all-start.1 = ((bf16[8,16,4608]{2,1,0:T(8,128)(2,1)}), bf16[8,16,4608]{2,1,0:T(8,128)(2,1)S(1)}, u32[]{:S(2)}, u32[]{:S(2)}) async-start(bf16[8,16,4608]{2,1,0:T(8,128)(2,1)} %bitcast.8), calls=%async_computation.1 | async-start | bytes 2359296 | tf_op jit(solution)/shard_map/all_to_all | solution.py:413
  119.8 4.0 %assemble1.1 = (f32[16,128]{1,0:T(8,128)S(1)}, f32[32,512]{1,0:T(8,128)S(1)}, f32[32,4096]{1,0:T(8,128)S(1)}) custom-call(s32[14,4096]{1,0:T(8,128)S(1)} %copy-done, f32[7,4608]{1,0:T(8,128)S(1)} %copy-done.1, f32[32,4096]{1,0:T(8,128)S(1)} %get-tuple-element.23.refs_2_, f32[32,4096]{1,0:T(8,128)S(1)} %get-tuple-element.24.refs_3_), custom_call_target="tpu_custom_call" | custom-call | flops 2000000000 | bytes 4000000 | tf_op jit(solution)/shard_map/assemble1/pallas_call | solution.py:170
  123.8 68.0 %level1.1 = (f32[16,4096]{1,0:T(8,128)S(1)}, f32[16,4096]{1,0:T(8,128)S(1)}) custom-call(f32[16,128]{1,0:T(8,128)S(1)} %get-tuple-element.25.refs_0_, f32[32,512]{1,0:T(8,128)S(1)} %get-tuple-element.26.refs_1_, f32[32,4096]{1,0:T(8,128)S(1)} %get-tuple-element.27.refs_2_), custom_call_target="tpu_custom_call" | custom-call | flops 30000001024 | bytes 150000000 | tf_op jit(solution)/shard_map/level1/pallas_call | solution.py:354
  191.9 0.2 convert_reduce_fusion.refs_4_
  192.0 0.0 copy-start.2
  192.0 3.8 %assemble2.1 = (f32[8,128]{1,0:T(8,128)S(1)}, f32[16,512]{1,0:T(8,128)S(1)}, f32[16,4096]{1,0:T(8,128)S(1)}) custom-call(s32[14,4096]{1,0:T(8,128)S(1)} %copy-done, f32[7,4608]{1,0:T(8,128)S(1)} %copy-done.1, f32[16,4096]{1,0:T(8,128)S(1)} %get-tuple-element.28.refs_2_, f32[16,4096]{1,0:T(8,128)S(1)} %get-tuple-element.29.refs_3_, ...), custom_call_target="tpu_custom_call" | custom-call | flops 2000000000 | bytes 4000000 | tf_op jit(solution)/shard_map/assemble2/pallas_call | solution.py:170
  195.8 47.1 %level2.1 = (f32[16,4096]{1,0:T(8,128)S(1)}, bf16[16,512]{1,0:T(8,128)(2,1)S(1)}) custom-call(f32[8,128]{1,0:T(8,128)S(1)} %get-tuple-element.31.refs_0_, f32[16,512]{1,0:T(8,128)S(1)} %get-tuple-element.32.refs_1_, f32[16,4096]{1,0:T(8,128)S(1)} %get-tuple-element.33.refs_2_, s32[1,512]{1,0:T(1,128)S(1)} %bitcast.6), custom_call_target="tpu_custom_call" | custom-call | flops 30000001024 | bytes 150000000 | tf_op jit(solution)/shard_map/level2/pallas_call | solution.py:354
  243.0 0.6 copy.11
  243.6 0.7 copy.12
  (7 shorter events, 0.0 us)
Async XLA Ops:
  7.7 8.8 %copy-start.3 = (f32[128,4096]{1,0:T(8,128)S(1)}, f32[128,4096]{1,0:T(8,128)}, u32[]{:S(2)}) copy-start(f32[128,4096]{1,0:T(8,128)} %param.7) | copy-start | bytes 6291460
  7.7 99.6 %all-to-all-start = ((bf16[32,16,4736]{2,1,0:T(8,128)(2,1)}), bf16[32,16,4736]{2,1,0:T(8,128)(2,1)}, u32[]{:S(2)}, u32[]{:S(2)}) async-start(bf16[32,16,4736]{2,1,0:T(8,128)(2,1)} %bitcast.7), calls=%async_computation | async-start | bytes 9699328 | tf_op jit(solution)/shard_map/all_to_all | solution.py:401
  16.5 14.4 %copy-start = (s32[14,4096]{1,0:T(8,128)S(1)}, s32[14,4096]{1,0:T(8,128)}, u32[]{:S(2)}) copy-start(s32[14,4096]{1,0:T(8,128)} %refs_0_.5) | copy-start | bytes 688132
  16.5 14.4 %copy-start.1 = (f32[7,4608]{1,0:T(8,128)S(1)}, f32[7,4608]{1,0:T(8,128)}, u32[]{:S(2)}) copy-start(f32[7,4608]{1,0:T(8,128)} %refs_1_.5) | copy-start | bytes 387076
  16.6 14.3 %collective-permute-start = (bf16[64,4096]{1,0:T(8,128)(2,1)S(1)}, bf16[64,4096]{1,0:T(8,128)(2,1)S(1)}, u32[]{:S(2)}, u32[]{:S(2)}) collective-permute-start(bf16[64,4096]{1,0:T(8,128)(2,1)S(1)} %slice.25), channel_id=1, source_target_pairs={{0,32},{4,36},{8,40},{12,44},{16,48},{20,52},{24,56},{28,60},{32,0... | collective-permute-start | bytes 1572872 | tf_op jit(solution)/shard_map/ppermute | solution.py:378
  111.6 80.3 %all-to-all-start.1 = ((bf16[8,16,4608]{2,1,0:T(8,128)(2,1)}), bf16[8,16,4608]{2,1,0:T(8,128)(2,1)S(1)}, u32[]{:S(2)}, u32[]{:S(2)}) async-start(bf16[8,16,4608]{2,1,0:T(8,128)(2,1)} %bitcast.8), calls=%async_computation.1 | async-start | bytes 2359296 | tf_op jit(solution)/shard_map/all_to_all | solution.py:413
  192.0 3.8 %copy-start.2 = (s32[512]{0:T(512)S(1)}, s32[512]{0:T(512)}, u32[]{:S(2)}) copy-start(s32[512]{0:T(512)} %param.10) | copy-start | bytes 6148
